TPU v7x, 256 devices: a whole 4x4x8 slice. The times are simulated.
256 devices in a mesh: dp: 32 (over y, z_hi, core), ctx: 8 (over x, z_lo).
Axes of the slice: x: 4, y: 4, z: 8 (z_hi: 4, z_lo: 2; z = z_hi * 2 + z_lo), core: 2. Of those that a mesh axis runs over, the one named last changes fastest.
Arguments:
- events: bfloat16 [65536, 512], P(('dp', 'ctx')), may hold values from -24 to 24
- out_grad: bfloat16 [65536, 512], P(('dp', 'ctx')), may hold values from -6 to 6
- proj_weight: bfloat16 [512, 2048], replicated, may hold values from -0.25 to 0.25
- out_weight: bfloat16 [512, 512], replicated, may hold values from -0.25 to 0.25
- lengths: int32 [32, 4], P('dp'), may hold values from 1 to 1024, 2048 in all within a row
- tile_mask: int32 [512, 16], P('dp'), may hold values 0 or 1
- quotient_shard: int32 [65536], P(('dp', 'ctx')), may hold values from 0 to 255, as said below
- quotient_row: int32 [65536], P(('dp', 'ctx')), may hold values from 0 to 65535
- remainder_shard: int32 [65536], P(('dp', 'ctx')), may hold values from 0 to 255, as said below
- remainder_row: int32 [65536], P(('dp', 'ctx')), may hold values from 0 to 65535
Outputs:
- quotient_grads: float32 [131072, 512], P(('dp', 'ctx'))
- remainder_grads: float32 [131072, 512], P(('dp', 'ctx'))
- proj_weight_grad: float32 [512, 2048], replicated
- out_weight_grad: float32 [512, 512], replicated
Inputs may be any that keep to these rules, and one draw needn't show every extreme that they name: `quotient_shard`: in every device's 256 rows no shard is named more than 2 times, and some shard exactly 2 times. `remainder_shard`: in every device's 256 rows no shard is named more than 2 times, and some shard exactly 2 times.
All inputs are finite; a program needn't handle non-finite values. No bound on the sum of `tile_mask` on one device may be relied on, other than what follows from the above.
Results may differ from a plain program's by a relative error of at most 0.0068.
Values may be sent and summed in bfloat16 or wider, within the bound.
No kernel may reach another device: no remote copies, remote signals or barrier semaphores. Data moves between devices by JAX's collectives and lax.ppermute only.
A program may use at most 128 MiB of HBM per device.

v0:
```python
import jax
import jax.numpy as jnp
from jax import lax
from jax.experimental import pallas as pl
from jax.experimental.pallas import tpu as pltpu
from jax.sharding import PartitionSpec as P

HEADS = 8
HD = 64
D = 512
TILE = 128
TOK = 256
LEN = 2048
NT = 16
NB = 8
LMAX = 1024
CAP = 2
DEVICES = 256
EPSILON = 1e-05
FAR = 1 << 30
BF = jnp.bfloat16
F32 = jnp.float32
MEMORY = 50 * 1024 * 1024

NN = (((1,), (0,)), ((), ()))
NT_DIMS = (((1,), (1,)), ((), ()))


def mm(a, b, dims=NN):
    return lax.dot_general(a, b, dims, preferred_element_type=F32)


def call(kernel, outs, scratch=(), smem=0, n_in=0):
    specs = [pl.BlockSpec(memory_space=pltpu.SMEM)] * smem + [
        pl.BlockSpec(memory_space=pltpu.VMEM)
    ] * (n_in - smem)
    return pl.pallas_call(
        kernel,
        out_shape=outs,
        in_specs=specs,
        out_specs=jax.tree.map(lambda _: pl.BlockSpec(memory_space=pltpu.VMEM), outs),
        scratch_shapes=list(scratch),
        compiler_params=pltpu.CompilerParams(vmem_limit_bytes=MEMORY),
    )


def out(shape, dtype):
    return jax.ShapeDtypeStruct(shape, dtype)


def send_kernel(ev_hbm, og_hbm, wo_hbm, out_ref, ev_s, og_s, wo_s, sems):
    copies = [
        pltpu.make_async_copy(src, dst, sems.at[i])
        for i, (src, dst) in enumerate(((og_hbm, og_s), (wo_hbm, wo_s), (ev_hbm, ev_s)))
    ]
    for copy in copies:
        copy.start()
    for copy in copies:
        copy.wait()
    gg = mm(wo_s[...], og_s[...], NT_DIMS).astype(BF)
    for h in range(HEADS):
        out_ref[h, :TOK, :] = ev_s[...]
        out_ref[h, TOK:, :TOK] = gg[HD * h : HD * h + 32]
        out_ref[h, TOK:, TOK:] = gg[HD * h + 32 : HD * h + 64]


def first_event(len_ref, position):
    e0 = len_ref[0]
    e1 = e0 + len_ref[1]
    e2 = e1 + len_ref[2]
    return jnp.where(
        position >= e2,
        e2,
        jnp.where(position >= e1, e1, jnp.where(position >= e0, e0, 0)),
    )


def seen(lo_ref, kb, k0, qs, row_pos):
    lower = jnp.concatenate(
        [
            jnp.broadcast_to(lo_ref[2 * kb, :, qs], (TILE, TOK)),
            jnp.broadcast_to(lo_ref[2 * kb + 1, :, qs], (TILE, TOK)),
        ],
        axis=0,
    )
    col_pos = k0 + lax.broadcasted_iota(jnp.int32, (TOK, TOK), 0)
    return (col_pos >= lower) & (col_pos <= row_pos)


def gate_cotangent(r_ref, s):
    return jnp.concatenate([r_ref[s, TOK:, :TOK], r_ref[s, TOK:, TOK:]], axis=0).astype(F32)


def forward_kernel(len_ref, r_ref, wt_ref, lo_ref, act_ref, ds_ref, mix_ref, out_ref, k_s, st_ref):
    for s in range(NB):
        cs = pl.ds(s * TOK, TOK)
        h = 0.5 * mm(wt_ref[...], r_ref[s, :TOK, :], NT_DIMS)
        t = jnp.tanh(h)
        u = h * t
        a = (h + u).astype(BF)
        act_ref[:, cs] = a
        ds_ref[:, cs] = (0.5 * (1.0 + t)) * (1.0 + (h - u))
        k_s[cs, :] = a[2 * HD : 3 * HD].T
    for qb in range(NB):
        qs = pl.ds(qb * TOK, TOK)
        qt = act_ref[:HD, qs] * BF(0.0625)
        row_pos = qb * TOK + lax.broadcasted_iota(jnp.int32, (1, TOK), 1)

        def step(kb, acc):
            k0 = pl.multiple_of(kb * TOK, TOK)
            h = mm(k_s[pl.ds(k0, TOK), :], qt)
            a = h + h * jnp.tanh(h)
            a = jnp.where(seen(lo_ref, kb, k0, qs, row_pos), a, 0.0).astype(BF)
            return acc + mm(act_ref[HD : 2 * HD, pl.ds(k0, TOK)], a)

        acc = lax.fori_loop(
            first_event(len_ref, qb * TOK) // TOK, qb + 1, step, jnp.zeros((HD, TOK), F32)
        )
        m = acc * (1.0 / LMAX)
        mix_ref[:, qs] = m
        s1 = jnp.sum(m, axis=0, keepdims=True)
        c = m - s1 * (1.0 / HD)
        gn = gate_cotangent(r_ref, qb) * act_ref[3 * HD :, qs].astype(F32)
        st_ref[0:1, qs] = s1
        st_ref[1:2, qs] = jnp.sum(c * c, axis=0, keepdims=True)
        st_ref[2:3, qs] = jnp.sum(gn, axis=0, keepdims=True)
        st_ref[3:4, qs] = jnp.sum(gn * c, axis=0, keepdims=True)
    for h in range(HEADS):
        out_ref[h] = st_ref[...]


def backward_kernel(
    len_ref, st_ref, r_ref, lo_ref, act_ref, ds_ref, mix_ref, lab_ref, gp_ref, gated_ref, k_s, v_s, dm_s, dv_s, dk_s
):
    gp_ref[:, 4 * HD :, :] = lab_ref[...]
    dv_s[...] = jnp.zeros((HD, LEN), F32)
    dk_s[...] = jnp.zeros((HD, LEN), F32)
    for s in range(NB):
        cs = pl.ds(s * TOK, TOK)
        v_s[cs, :] = act_ref[HD : 2 * HD, cs].T
        k_s[cs, :] = act_ref[2 * HD : 3 * HD, cs].T
        st = st_ref[:, :, cs]
        s1, m2, s3, s4 = st[:, 0], st[:, 1], st[:, 2], st[:, 3]
        mean = jnp.sum(s1, axis=0, keepdims=True) * (1.0 / D)
        apart = s1 * (1.0 / HD) - mean
        var = jnp.sum(m2 + HD * apart * apart, axis=0, keepdims=True) * (1.0 / D)
        inv = lax.rsqrt(var + EPSILON)
        mean_gn = jnp.sum(s3, axis=0, keepdims=True) * (1.0 / D)
        mean_gnn = jnp.sum(s4 + s3 * apart, axis=0, keepdims=True) * (1.0 / D) * inv
        normed = (mix_ref[:, cs] - mean) * inv
        gate = act_ref[3 * HD :, cs].astype(F32)
        gg = gate_cotangent(r_ref, s)
        gated_ref[:, cs] = (normed * gate).astype(BF)
        dm_s[:, cs] = (inv * (gg * gate - mean_gn - normed * mean_gnn)).astype(BF)
        gp_ref[s, 3 * HD : 4 * HD, :] = (gg * normed * ds_ref[3 * HD :, cs]).astype(BF)
    for qb in range(NB):
        qs = pl.ds(qb * TOK, TOK)
        qt = act_ref[:HD, qs] * BF(0.0625)
        dm = dm_s[:, qs]
        row_pos = qb * TOK + lax.broadcasted_iota(jnp.int32, (1, TOK), 1)

        def step(kb, acc):
            k0 = pl.multiple_of(kb * TOK, TOK)
            ks = pl.ds(k0, TOK)
            h = mm(k_s[ks, :], qt)
            da = mm(v_s[ks, :], dm)
            t = jnp.tanh(h)
            u = h * t
            vis = seen(lo_ref, kb, k0, qs, row_pos)
            a = jnp.where(vis, h + u, 0.0).astype(BF)
            d = jnp.where(vis, da * ((1.0 + t) * (1.0 + (h - u))), 0.0).astype(BF)
            dv_s[:, ks] += mm(dm, a, NT_DIMS)
            dk_s[:, ks] += mm(qt, d, NT_DIMS)
            return acc + mm(act_ref[2 * HD : 3 * HD, ks], d)

        acc = lax.fori_loop(
            first_event(len_ref, qb * TOK) // TOK, qb + 1, step, jnp.zeros((HD, TOK), F32)
        )
        gp_ref[qb, :HD, :] = (acc * (1.0 / (16 * LMAX)) * ds_ref[:HD, qs]).astype(BF)
    for s in range(NB):
        cs = pl.ds(s * TOK, TOK)
        gp_ref[s, HD : 2 * HD, :] = (dv_s[:, cs] * (1.0 / LMAX) * ds_ref[HD : 2 * HD, cs]).astype(BF)
        gp_ref[s, 2 * HD : 3 * HD, :] = (dk_s[:, cs] * (1.0 / LMAX) * ds_ref[2 * HD : 3 * HD, cs]).astype(BF)


def weight_kernel(place_ref, gp_ref, r_ref, gated_ref, *refs):
    ch_ref = refs[NB // 2]
    pw = jnp.zeros((4 * HD, D), F32)
    ow = jnp.zeros((HD, D), F32)
    for s in range(NB):
        pw = pw + mm(gp_ref[s, : 4 * HD], r_ref[s, :TOK, :])
        first = pl.multiple_of((place_ref[0] ^ s) * TOK, TOK)
        ow = ow + mm(gated_ref[:, pl.ds(first, TOK)], refs[s // 2][s % 2])
    pw = pw.T
    ch_ref[:D, :] = pw[:, :128]
    ch_ref[D : 2 * D, :] = pw[:, 128:]
    for c in range(4):
        ch_ref[2 * D + HD * c : 2 * D + HD * (c + 1), :] = ow[:, 128 * c : 128 * (c + 1)]


def pack_kernel(back_ref, w_ref, og_ref, tq_ref, tr_ref, out_ref, gp_s, row_s):
    for h in range(HEADS):
        for b, block in enumerate((2, 1, 3, 0)):
            gp_s[D * block + HD * h : D * block + HD * (h + 1), :] = back_ref[h, HD * b : HD * (b + 1), :]
    ge = (mm(w_ref[...], gp_s[...]).T + og_ref[...].astype(F32)).astype(BF)
    shard = lax.broadcasted_iota(jnp.int32, (DEVICES, TOK), 0)
    for t, target_ref in enumerate((tq_ref, tr_ref)):
        for k in range(CAP):
            pick = (target_ref[...] == CAP * shard + k).astype(F32).astype(BF)
            rows = mm(pick, ge)
            for c in range(4):
                row_s[pl.ds(8 * t + 4 * k + c, DEVICES, stride=16), :] = rows[:, 128 * c : 128 * (c + 1)]
    out_ref[...] = row_s[...].astype(BF).reshape(DEVICES, 16, 128)


def merge_kernel(in_ref, qc_ref, qr_ref, rc_ref, rr_ref, q_ref, r_ref, row_s):
    row_s[...] = in_ref[...].reshape(DEVICES * 16, 128).astype(F32)
    for t, (col_ref, mark_ref, o_ref) in enumerate(((qc_ref, qr_ref, q_ref), (rc_ref, rr_ref, r_ref))):
        same = (col_ref[...] == mark_ref[...]) & (mark_ref[...] >= 0)
        same = same.astype(F32).astype(BF)
        rows = jnp.concatenate(
            [
                jnp.concatenate(
                    [row_s[pl.ds(8 * t + 4 * k + c, DEVICES, stride=16), :] for c in range(4)], axis=1
                )
                for k in range(CAP)
            ],
            axis=0,
        ).astype(BF)
        o_ref[...] = mm(same, rows)


def place_kernel(place_ref, *refs):
    for k in range(HEADS):
        refs[HEADS][place_ref[0] ^ k] = refs[k][...]


def weights_out_kernel(core_ref, mine_ref, other_ref, pw_ref, ow_ref):
    step = pl.program_id(0)
    left = lax.broadcasted_iota(jnp.int32, (128, 128), 1) < HD

    def write(low_ref, high_ref):
        def write_part(part, get):
            low, high = ((2, 1), (3, 0))[part]
            for h in range(0, HEADS, 2):
                a, b = get(h), get(h + 1)
                pw_ref[:, D * low + HD * h : D * low + HD * h + 128] = jnp.where(left, a, pltpu.roll(b, HD, 1))
                pw_ref[:, D * high + HD * h : D * high + HD * h + 128] = jnp.where(left, pltpu.roll(a, HD, 1), b)

        first = pl.multiple_of(step * 128, 128)
        write_part(0, lambda h: low_ref[h, pl.ds(first, 128), :].astype(F32))

        @pl.when(step == 0)
        def _():
            write_part(1, lambda h: low_ref[h, D:640, :].astype(F32))

        @pl.when(step != 0)
        def _():
            after = pl.multiple_of(jnp.maximum(step - 1, 0) * 128, 128)
            write_part(1, lambda h: high_ref[h, pl.ds(after, 128), :].astype(F32))

        for i in range(2):
            for c in range(4):
                ow_ref[HD * i : HD * (i + 1), 128 * c : 128 * (c + 1)] = high_ref[
                    2 * step + i, 384 + HD * c : 384 + HD * (c + 1), :
                ].astype(F32)

    @pl.when(core_ref[0] == 0)
    def _():
        write(mine_ref, other_ref)

    @pl.when(core_ref[0] != 0)
    def _():
        write(other_ref, mine_ref)


def turned(stride, size, by, count=32):
    pairs = []
    for i in range(count):
        digit = (i // stride) % size
        pairs.append((i, i + ((digit + by) % size - digit) * stride))
    return pairs


def scatter_sum(x, stride):
    parts = x.reshape(4, x.shape[0] // 4, 128)
    me = (lax.axis_index("dp") // stride) % 4
    total = lax.dynamic_index_in_dim(parts, me, 0, False)
    for k in (1, 2, 3):
        sent = lax.dynamic_index_in_dim(parts, (me + k) % 4, 0, False)
        total = total + lax.ppermute(sent, "dp", turned(stride, 4, k))
    return total


def total(x, stride):
    return x + sum(lax.ppermute(x, "dp", turned(stride, 4, k)) for k in (1, 2, 3))


def by_source(parts, stride, size):
    me = (lax.axis_index("dp") // stride) % size
    held = [lax.dynamic_index_in_dim(parts, me, 0, False)]
    for k in range(1, size):
        sent = lax.dynamic_index_in_dim(parts, (me + k) % size, 0, False)
        held.append(lax.ppermute(sent, "dp", turned(stride, size, k)))
    back = jnp.stack([held[-i % size] for i in range(size)] * 2)
    return lax.dynamic_slice_in_dim(back, (size - me) % size, size, 0)


def gathered(x, stride):
    return by_source(jnp.broadcast_to(x[None], (4,) + x.shape), stride, 4).reshape(-1, 128)


def labels_over_dp(labels):
    x = labels.reshape(4, 4, 2, 32)
    x = by_source(x.transpose(2, 0, 1, 3), 1, 2)
    x = by_source(x.transpose(1, 0, 2, 3), 8, 4)
    x = by_source(x.transpose(2, 0, 1, 3), 2, 4)
    return x.transpose(1, 0, 2, 3)


def label_digits(x):
    x = x.reshape(32, 8, 4).transpose(1, 0, 2).reshape(8, 128)
    x = jnp.concatenate([(x + 1) // 256, (x + 1) % 256], axis=1)
    return jnp.broadcast_to(x[:, None], (8, 16, 256)).astype(BF)


def over_ctx(x, k):
    return lax.ppermute(x, "ctx", [(i, i ^ k) for i in range(8)])


def together(*arrays):
    return lax.optimization_barrier(arrays)


def core_sum(terms):
    core = lax.axis_index("dp") % 2
    halves = terms.reshape(2, 640, 128)
    mine = lax.dynamic_index_in_dim(halves, core, 0, False)
    other = lax.dynamic_index_in_dim(halves, 1 - core, 0, False)
    return mine + lax.ppermute(other, "dp", turned(1, 2, 1))


def weights_out(mine):
    core = lax.axis_index("dp") % 2
    other = lax.ppermute(mine, "dp", turned(1, 2, 1))
    whole = pl.BlockSpec((HEADS, 640, 128), lambda i: (0, 0, 0))
    return pl.pallas_call(
        weights_out_kernel,
        out_shape=(out((D, 4 * D), F32), out((D, D), F32)),
        grid=(4,),
        in_specs=[pl.BlockSpec(memory_space=pltpu.SMEM), whole, whole],
        out_specs=(pl.BlockSpec((128, 4 * D), lambda i: (i, 0)), pl.BlockSpec((128, D), lambda i: (i, 0))),
        compiler_params=pltpu.CompilerParams(vmem_limit_bytes=MEMORY),
    )(core.reshape(1).astype(jnp.int32), mine, other)


def slot_targets(shards):
    order = jnp.arange(TOK)
    earlier = (shards[:, None] == shards[None, :]) & (order[:, None] < order[None, :])
    return shards * CAP + jnp.sum(earlier.astype(jnp.int32), axis=0)


def slot_labels(target, rows):
    onehot = jnp.arange(DEVICES * CAP, dtype=jnp.int32)[:, None] == target[None, :]
    labels = jnp.sum(jnp.where(onehot, rows[None, :] + 1, 0), axis=1) - 1
    return labels.reshape(DEVICES, CAP)


def body(
    events,
    out_grad,
    proj_weight,
    out_weight,
    lengths,
    tile_mask,
    quotient_shard,
    quotient_row,
    remainder_shard,
    remainder_row,
):
    history = lengths[0]
    head = lax.axis_index("ctx")

    sent = pl.pallas_call(
        send_kernel,
        out_shape=out((HEADS, TOK + 32, D), BF),
        in_specs=[pl.BlockSpec(memory_space=pl.ANY)] * 3,
        out_specs=pl.BlockSpec(memory_space=pltpu.VMEM),
        scratch_shapes=[
            pltpu.VMEM((TOK, D), BF),
            pltpu.VMEM((TOK, D), BF),
            pltpu.VMEM((D, D), BF),
            pltpu.SemaphoreType.DMA((3,)),
        ],
        compiler_params=pltpu.CompilerParams(vmem_limit_bytes=MEMORY),
    )(events, out_grad, out_weight)
    sent, quotient_shard, remainder_shard = together(sent, quotient_shard, remainder_shard)
    received = lax.all_to_all(sent, "ctx", 0, 0, tiled=True)

    own = lax.dynamic_index_in_dim(proj_weight.reshape(D, 4, HEADS, HD), head, 2, False)
    own_t = jnp.stack([own[:, b].T for b in (2, 1, 3, 0)]).reshape(4 * HD, D)
    position = jnp.arange(LEN, dtype=jnp.int32)
    end0 = history[0]
    end1 = end0 + history[1]
    end2 = end1 + history[2]
    first = jnp.where(
        position >= end2,
        end2,
        jnp.where(position >= end1, end1, jnp.where(position >= end0, end0, 0)),
    )
    kept = jnp.repeat(tile_mask.T, TILE, axis=1) > 0
    lower = jnp.where(kept, first[None, :], FAR).reshape(NT, 1, LEN)

    quotient_target = slot_targets(quotient_shard)
    remainder_target = slot_targets(remainder_shard)
    labels = jnp.concatenate(
        [slot_labels(quotient_target, quotient_row), slot_labels(remainder_target, remainder_row)], axis=1
    )
    labels = labels_over_dp(labels)
    beside = over_ctx(out_grad, 1)
    received, beside = together(received, beside)
    grad_pair = jnp.stack([out_grad, beside])
    far_pair = over_ctx(grad_pair, 4)

    act, slope, mixed, stats = call(
        forward_kernel,
        (out((4 * HD, LEN), BF), out((4 * HD, LEN), F32), out((HD, LEN), F32), out((HEADS, 4, LEN), F32)),
        [pltpu.VMEM((LEN, HD), BF), pltpu.VMEM((4, LEN), F32)],
        smem=1,
        n_in=4,
    )(history, received, own_t, lower)
    stats, labels = together(stats, labels)
    all_stats = lax.all_to_all(stats, "ctx", 0, 0, tiled=True)
    labels = label_digits(labels)
    all_stats, grad_pair = together(all_stats, grad_pair)
    group_grad = [grad_pair, over_ctx(grad_pair, 2), far_pair, over_ctx(grad_pair, 6)]
    grads, gated = call(
        backward_kernel,
        (out((NB, 4 * HD + 16, TOK), BF), out((HD, LEN), BF)),
        [
            pltpu.VMEM((LEN, HD), BF),
            pltpu.VMEM((LEN, HD), BF),
            pltpu.VMEM((HD, LEN), BF),
            pltpu.VMEM((HD, LEN), F32),
            pltpu.VMEM((HD, LEN), F32),
        ],
        smem=1,
        n_in=8,
    )(history, all_stats, received, lower, act, slope, mixed, labels)
    grads, *group_grad = together(grads, *group_grad)

    back = lax.all_to_all(grads, "ctx", 0, 0, tiled=True)
    marks = back[:, 4 * HD].astype(F32).astype(jnp.int32)
    marks = marks[:, :128] * 256 + marks[:, 128:] - 1
    marks = marks.reshape(8, 32, 4).transpose(1, 0, 2).reshape(DEVICES, 2, CAP)
    terms = call(weight_kernel, out((1280, 128), F32), smem=1, n_in=8)(
        head.reshape(1).astype(jnp.int32), grads, received, gated, *group_grad
    )
    terms = scatter_sum(core_sum(terms), 8)
    back, terms = together(back, terms)
    terms = total(terms, 2)
    packed = call(
        pack_kernel,
        out((DEVICES, 16, 128), BF),
        [pltpu.VMEM((4 * D, TOK), BF), pltpu.VMEM((DEVICES * 16, 128), F32)],
        n_in=5,
    )(back, proj_weight, out_grad, quotient_target.reshape(1, TOK), remainder_target.reshape(1, TOK))
    packed, terms = together(packed, terms)
    arrived = lax.all_to_all(packed, ("dp", "ctx"), 0, 0, tiled=True)
    terms = gathered(terms, 8).astype(BF)
    columns = [marks[:, t].reshape(DEVICES * CAP, 1) for t in range(2)]
    rows = [marks[:, t].T.reshape(1, DEVICES * CAP) for t in range(2)]
    quotient_grads, remainder_grads = call(
        merge_kernel,
        (out((DEVICES * CAP, D), F32), out((DEVICES * CAP, D), F32)),
        [pltpu.VMEM((DEVICES * 16, 128), F32)],
        n_in=5,
    )(arrived, columns[0], rows[0], columns[1], rows[1])
    held = [terms] + [over_ctx(terms, k) for k in range(1, 8)]
    quotient_grads, *held = together(quotient_grads, *held)
    terms = call(place_kernel, out((HEADS, 640, 128), BF), smem=1, n_in=9)(head.reshape(1).astype(jnp.int32), *held)
    proj_weight_grad, out_weight_grad = weights_out(terms)
    return (quotient_grads, remainder_grads, proj_weight_grad, out_weight_grad)


def solution(mesh):
    split = P(("dp", "ctx"))
    in_specs = (
        P(("dp", "ctx"), None),
        P(("dp", "ctx"), None),
        P(),
        P(),
        P("dp", None),
        P("dp", None),
        split,
        split,
        split,
        split,
    )
    out_specs = (P(("dp", "ctx"), None), P(("dp", "ctx"), None), P(), P())
    return jax.shard_map(body, mesh=mesh, in_specs=in_specs, out_specs=out_specs, check_vma=False)
```

profile of v0, /device:TPU:1, one launch (start us, length us, event | category | flops | bytes accessed | tf_op | source)
XLA Modules:
  0.0 186.3 jit_solution(10666776735328689555)
XLA Ops:
  0.6 2.6 %collective-permute-start = (bf16[256,512]{1,0:T(8,128)(2,1)}, bf16[256,512]{1,0:T(8,128)(2,1)S(1)}, u32[]{:S(2)}, u32[]{:S(2)}) collective-permute-start(bf16[256,512]{1,0:T(8,128)(2,1)} %og_ref.1), channel_id=1, source_target_pairs={{0,1},{1,0},{2,3},{3,2},{4,5},{5,4},{6,7},{7,6},{8,9},{9,8},{10,11... | collective-permute-start | bytes 786440 | tf_op jit(solution)/shard_map/ppermute | solution.py:328
  3.2 1.0 copy-done
  4.2 1.0 copy-done.6
  5.2 0.9 copy-done.9
  6.2 1.9 %shard_map.129 = bf16[8,288,512]{2,1,0:T(8,128)(2,1)} custom-call(bf16[256,512]{1,0:T(8,128)(2,1)S(1)} %copy-done.9, bf16[256,512]{1,0:T(8,128)(2,1)S(1)} %copy-done, bf16[512,512]{1,0:T(8,128)(2,1)S(1)} %copy-done.6), custom_call_target="tpu_custom_call" | custom-call | tf_op jit(solution)/shard_map/pallas_call | solution.py:384
  8.2 4.5 %all-to-all-start = ((bf16[8,288,512]{2,1,0:T(8,128)(2,1)}), bf16[8,288,512]{2,1,0:T(8,128)(2,1)}, u32[]{:S(2)}, u32[]{:S(2)}) async-start(bf16[8,288,512]{2,1,0:T(8,128)(2,1)} %shard_map.129), calls=%async_computation | async-start | bytes 4718592 | tf_op jit(solution)/shard_map/all_to_all | solution.py:398
  12.9 0.1 select_reduce_fusion.1
  13.1 0.1 select_reduce_fusion
  13.8 1.0 collective-permute-start.1
  14.8 0.6 fusion.14
  15.7 2.5 %copy.64 = bf16[512,2048]{0,1:T(8,128)(2,1)} copy(bf16[512,2048]{1,0:T(8,128)(2,1)S(1)} %copy-done.11) | data formatting | bytes 4194304 | tf_op args[2]
  18.2 1.0 dynamic-slice_bitcast_fusion.1
  21.2 0.7 select_select_fusion
  21.9 0.2 broadcast_select_fusion.lo_ref
  22.3 1.4 collective-permute-start.4
  23.7 2.6 %collective-permute-start.3 = (s32[2,4,32]{2,1,0:T(4,128)S(1)}, s32[2,4,32]{2,1,0:T(4,128)S(1)}, u32[]{:S(2)}, u32[]{:S(2)}) collective-permute-start(s32[2,4,32]{2,1,0:T(4,128)S(1)} %get-tuple-element.90), channel_id=1, source_target_pairs={{0,128},{8,136},{16,144},{24,152},{32,160},{40,168},{48,176},{56,1... | collective-permute-start | bytes 3080 | tf_op jit(solution)/shard_map/ppermute | solution.py:304
  26.3 1.1 collective-permute-start.2
  27.4 1.8 collective-permute-done.2
  29.3 6.4 %collective-permute-start.6 = (s32[4,2,32]{2,1,0:T(2,128)S(1)}, s32[4,2,32]{2,1,0:T(2,128)S(1)}, u32[]{:S(2)}, u32[]{:S(2)}) collective-permute-start(s32[4,2,32]{2,1,0:T(2,128)S(1)} %bitcast.170), channel_id=1, source_target_pairs={{0,32},{8,40},{16,48},{24,56},{32,0},{40,8},{48,16},{56,24},{64,96... | collective-permute-start | bytes 3080 | tf_op jit(solution)/shard_map/ppermute | solution.py:304
  35.7 1.2 collective-permute-start.7
  36.9 2.4 %collective-permute-start.5 = (s32[4,2,32]{2,1,0:T(2,128)S(1)}, s32[4,2,32]{2,1,0:T(2,128)S(1)}, u32[]{:S(2)}, u32[]{:S(2)}) collective-permute-start(s32[4,2,32]{2,1,0:T(2,128)S(1)} %bitcast.171), channel_id=1, source_target_pairs={{0,48},{8,56},{16,0},{24,8},{32,16},{40,24},{48,32},{56,40},{64,11... | collective-permute-start | bytes 3080 | tf_op jit(solution)/shard_map/ppermute | solution.py:304
  39.3 1.4 collective-permute-done.5
  40.7 3.6 %collective-permute-done.6 = s32[4,2,32]{2,1,0:T(2,128)S(1)} collective-permute-done((s32[4,2,32]{2,1,0:T(2,128)S(1)}, s32[4,2,32]{2,1,0:T(2,128)S(1)}, u32[]{:S(2)}, u32[]{:S(2)}) %collective-permute-start.6) | collective-permute-done | bytes 1056 | tf_op jit(solution)/shard_map/ppermute | solution.py:304
  44.3 0.7 copy-done.12
  45.0 10.7 %shard_map.130 = (bf16[256,2048]{1,0:T(8,128)(2,1)S(1)}, f32[256,2048]{1,0:T(8,128)}, f32[64,2048]{1,0:T(8,128)S(1)}, f32[8,4,2048]{2,1,0:T(4,128)}) custom-call(s32[4]{0:T(128)S(1)} %bitcast.150, bf16[8,288,512]{2,1,0:T(8,128)(2,1)} %all-to-all-done.r_ref, bf16[256,512]{1,0:T(8,128)(2,1)S(1)} %bitcast.141, s32[16,1,2048]{2,1,0:T(1,128)S(1)} %broadcast_select_fusion.lo_ref), custom_call_target="tpu_custom_call" | custom-call | tf_op jit(solution)/shard_map/pallas_call | solution.py:425
  55.7 0.8 copy-done.4
  56.5 5.2 %all-to-all-start.1 = ((f32[8,4,2048]{2,1,0:T(4,128)}), f32[8,4,2048]{2,1,0:T(4,128)S(1)}, u32[]{:S(2)}, u32[]{:S(2)}) async-start(f32[8,4,2048]{2,1,0:T(4,128)} %get-tuple-element.46), calls=%async_computation.1 | async-start | bytes 524288 | tf_op jit(solution)/shard_map/all_to_all | solution.py:433
  61.7 3.0 %collective-permute-start.9 = (bf16[2,256,512]{2,1,0:T(8,128)(2,1)S(1)}, bf16[2,256,512]{2,1,0:T(8,128)(2,1)S(1)}, u32[]{:S(2)}, u32[]{:S(2)}) collective-permute-start(bf16[2,256,512]{2,1,0:T(8,128)(2,1)S(1)} %pad_maximum_fusion.refs_0_), channel_id=1, source_target_pairs={{0,4},{1,5},{2,6},{3,7},{4,0},{5,1},{6,2},{7,3},{8,12},{9,13},{10,... | collective-permute-start | bytes 1572872 | tf_op jit(solution)/shard_map/ppermute | solution.py:328
  64.8 3.3 %all-to-all-done.1.st_ref = f32[8,4,2048]{2,1,0:T(4,128)S(1)} async-done(((f32[8,4,2048]{2,1,0:T(4,128)}), f32[8,4,2048]{2,1,0:T(4,128)S(1)}, u32[]{:S(2)}, u32[]{:S(2)}) %all-to-all-start.1) | async-done | bytes 262176 | tf_op jit(solution)/shard_map/all_to_all | solution.py:433
  68.1 0.3 collective-permute-start.10
  68.5 0.3 copy.67
  68.9 1.0 copy-done.5
  70.0 11.8 %shard_map.131 = (bf16[8,272,256]{2,1,0:T(8,128)(2,1)}, bf16[64,2048]{1,0:T(8,128)(2,1)S(1)}) custom-call(s32[4]{0:T(128)S(1)} %bitcast.151, f32[8,4,2048]{2,1,0:T(4,128)S(1)} %all-to-all-done.1.st_ref, bf16[8,288,512]{2,1,0:T(8,128)(2,1)} %all-to-all-done.r_ref, s32[16,1,2048]{2,1,0:T(1,128)S(1)} %broadcast_select_fusion.lo_ref, ...), custom_call_target="tpu_custom_call" | custom-call | tf_op jit(solution)/shard_map/pallas_call | solution.py:437
  81.8 0.7 copy-done.7
  82.5 8.0 %collective-permute-done.10.refs_3_ = bf16[2,256,512]{2,1,0:T(8,128)(2,1)S(1)} collective-permute-done((bf16[2,256,512]{2,1,0:T(8,128)(2,1)S(1)}, bf16[2,256,512]{2,1,0:T(8,128)(2,1)S(1)}, u32[]{:S(2)}, u32[]{:S(2)}) %collective-permute-start.10) | collective-permute-done | bytes 524320 | tf_op jit(solution)/shard_map/ppermute | solution.py:328
  90.5 0.8 copy-done.2
  91.3 3.7 %all-to-all-start.2 = ((bf16[8,272,256]{2,1,0:T(8,128)(2,1)}), bf16[8,272,256]{2,1,0:T(8,128)(2,1)S(1)}, u32[]{:S(2)}, u32[]{:S(2)}) async-start(bf16[8,272,256]{2,1,0:T(8,128)(2,1)} %get-tuple-element.55.gp_ref), calls=%async_computation.2 | async-start | bytes 2228224 | tf_op jit(solution)/shard_map/all_to_all | solution.py:452
  95.0 3.3 %shard_map.132 = f32[1280,128]{1,0:T(8,128)S(1)} custom-call(s32[1]{0:T(128)} %bitcast.42.place_ref, bf16[8,272,256]{2,1,0:T(8,128)(2,1)} %get-tuple-element.55.gp_ref, bf16[8,288,512]{2,1,0:T(8,128)(2,1)} %all-to-all-done.r_ref, bf16[64,2048]{1,0:T(8,128)(2,1)S(1)} %copy-done.8, bf16[2,256,512]{2,1,0:T(8,128)(2,1)S(1)} %pad_maximum_fusion.refs_0_, ...), custom_call_target="tpu_custom_call" | custom-call | tf_op jit(solution)/shard_map/pallas_call | solution.py:456
  98.3 5.8 %collective-permute-start.11 = (f32[640,128]{1,0:T(8,128)S(1)}, f32[640,128]{1,0:T(8,128)S(1)}, u32[]{:S(2)}, u32[]{:S(2)}) collective-permute-start(f32[640,128]{1,0:T(8,128)S(1)} %dynamic-slice_bitcast_fusion), channel_id=1, source_target_pairs={{0,8},{8,0},{16,24},{24,16},{32,40},{40,32},{48,56},{56,48},{64,72... | collective-permute-start | bytes 983048 | tf_op jit(solution)/shard_map/ppermute | solution.py:340
  104.1 1.3 collective-permute-done.11
  105.4 0.6 collective-permute-start.12
  106.1 2.1 %collective-permute-start.14 = (f32[160,128]{1,0:T(8,128)S(1)}, f32[160,128]{1,0:T(8,128)S(1)}, u32[]{:S(2)}, u32[]{:S(2)}) collective-permute-start(f32[160,128]{1,0:T(8,128)S(1)} %get-tuple-element.79), channel_id=1, source_target_pairs={{0,192},{8,200},{16,208},{24,216},{32,224},{40,232},{48,240},{56,2... | collective-permute-start | bytes 245768 | tf_op jit(solution)/shard_map/ppermute | solution.py:291
  108.2 3.6 %collective-permute-start.13 = (f32[160,128]{1,0:T(8,128)S(1)}, f32[160,128]{1,0:T(8,128)S(1)}, u32[]{:S(2)}, u32[]{:S(2)}) collective-permute-start(f32[160,128]{1,0:T(8,128)S(1)} %get-tuple-element.80), channel_id=1, source_target_pairs={{0,128},{8,136},{16,144},{24,152},{32,160},{40,168},{48,176},{56,1... | collective-permute-start | bytes 245768 | tf_op jit(solution)/shard_map/ppermute | solution.py:291
  111.8 0.4 collective-permute-done.14
  112.2 2.1 %collective-permute-done.13 = f32[160,128]{1,0:T(8,128)S(1)} collective-permute-done((f32[160,128]{1,0:T(8,128)S(1)}, f32[160,128]{1,0:T(8,128)S(1)}, u32[]{:S(2)}, u32[]{:S(2)}) %collective-permute-start.13) | collective-permute-done | bytes 81952 | tf_op jit(solution)/shard_map/ppermute | solution.py:291
  114.4 3.1 %collective-permute-start.16 = (f32[160,128]{1,0:T(8,128)S(1)}, f32[160,128]{1,0:T(8,128)S(1)}, u32[]{:S(2)}, u32[]{:S(2)}) collective-permute-start(f32[160,128]{1,0:T(8,128)S(1)} %fusion.3), channel_id=1, source_target_pairs={{0,32},{8,40},{16,48},{24,56},{32,0},{40,8},{48,16},{56,24},{64,96... | collective-permute-start | bytes 245768 | tf_op jit(solution)/shard_map/ppermute | solution.py:296
  117.5 1.0 collective-permute-start.15
  118.5 4.6 %shard_map.133 = bf16[256,16,128]{2,1,0:T(8,128)(2,1)} custom-call(bf16[8,272,256]{2,1,0:T(8,128)(2,1)S(1)} %all-to-all-done.2.back_ref, bf16[512,2048]{1,0:T(8,128)(2,1)} %w_ref.1, bf16[256,512]{1,0:T(8,128)(2,1)S(1)} %copy-done.1, s32[1,256]{1,0:T(1,128)S(1)} %bitcast.153, s32[1,256]{1,0:T(1,128)S(1)} %bitcast.152), custom_call_target="tpu_custom_call" | custom-call | tf_op jit(solution)/shard_map/pallas_call | solution.py:462
  123.0 1.9 collective-permute-done.15
  125.0 4.2 %collective-permute-start.19 = (bf16[160,128]{1,0:T(8,128)(2,1)S(1)}, bf16[160,128]{1,0:T(8,128)(2,1)S(1)}, u32[]{:S(2)}, u32[]{:S(2)}) collective-permute-start(bf16[160,128]{1,0:T(8,128)(2,1)S(1)} %add_add_fusion), channel_id=1, source_target_pairs={{0,128},{8,136},{16,144},{24,152},{32,160},{40,168},{48,176},{56,1... | collective-permute-start | bytes 122888 | tf_op jit(solution)/shard_map/ppermute | solution.py:304
  129.2 11.9 %all-to-all-start.3 = ((bf16[256,16,128]{2,1,0:T(8,128)(2,1)}), bf16[256,16,128]{2,1,0:T(8,128)(2,1)S(1)}, u32[]{:S(2)}, u32[]{:S(2)}) async-start(bf16[256,16,128]{2,1,0:T(8,128)(2,1)} %shard_map.133), calls=%async_computation.3 | async-start | bytes 2097152 | tf_op jit(solution)/shard_map/all_to_all | solution.py:469
  141.3 3.8 %collective-permute-start.27 = (bf16[640,128]{1,0:T(8,128)(2,1)S(1)}, bf16[640,128]{1,0:T(8,128)(2,1)S(1)}, u32[]{:S(2)}, u32[]{:S(2)}) collective-permute-start(bf16[640,128]{1,0:T(8,128)(2,1)S(1)} %bitcast.142), channel_id=1, source_target_pairs={{0,7},{1,6},{2,5},{3,4},{4,3},{5,2},{6,1},{7,0},{8,15},{9,14},{10,... | collective-permute-start | bytes 491528 | tf_op jit(solution)/shard_map/ppermute | solution.py:328
  145.0 0.2 collective-permute-start.26
  145.5 1.4 collective-permute-start.25
  146.9 1.5 collective-permute-start.24
  148.4 1.1 collective-permute-start.23
  149.5 20.7 %collective-permute-done.27.refs_7_ = bf16[640,128]{1,0:T(8,128)(2,1)S(1)} collective-permute-done((bf16[640,128]{1,0:T(8,128)(2,1)S(1)}, bf16[640,128]{1,0:T(8,128)(2,1)S(1)}, u32[]{:S(2)}, u32[]{:S(2)}) %collective-permute-start.27) | collective-permute-done | bytes 163872 | tf_op jit(solution)/shard_map/ppermute | solution.py:328
  170.8 2.7 %all-to-all-done.3.in_ref = bf16[256,16,128]{2,1,0:T(8,128)(2,1)S(1)} async-done(((bf16[256,16,128]{2,1,0:T(8,128)(2,1)}), bf16[256,16,128]{2,1,0:T(8,128)(2,1)S(1)}, u32[]{:S(2)}, u32[]{:S(2)}) %all-to-all-start.3) | async-done | bytes 1048608 | tf_op jit(solution)/shard_map/all_to_all | solution.py:469
  173.5 2.2 %shard_map.134 = (f32[512,512]{1,0:T(8,128)}, f32[512,512]{1,0:T(8,128)}) custom-call(bf16[256,16,128]{2,1,0:T(8,128)(2,1)S(1)} %all-to-all-done.3.in_ref, s32[512,1]{1,0:T(8,128)S(1)} %reshape_squeeze.8.qc_ref, s32[1,512]{1,0:T(1,128)S(1)} %bitcast.155, s32[512,1]{1,0:T(8,128)S(1)} %reshape_squeeze.9.rc_ref, s32[1,512]{1,0:T(1,128)S(1)} %bitcast.154), custom_call_target="tpu_custom_call" | custom-call | tf_op jit(solution)/shard_map/pallas_call | solution.py:473
  175.7 0.3 collective-permute-done.23.refs_3_
  176.0 3.8 %collective-permute-done.22.refs_2_ = bf16[640,128]{1,0:T(8,128)(2,1)S(1)} collective-permute-done((bf16[640,128]{1,0:T(8,128)(2,1)S(1)}, bf16[640,128]{1,0:T(8,128)(2,1)S(1)}, u32[]{:S(2)}, u32[]{:S(2)}) %collective-permute-start.22) | collective-permute-done | bytes 163872 | tf_op jit(solution)/shard_map/ppermute | solution.py:328
  179.9 0.6 collective-permute-start.28
  180.5 2.7 %collective-permute-done.28.other_ref = bf16[8,640,128]{2,1,0:T(8,128)(2,1)S(1)} collective-permute-done((bf16[8,640,128]{2,1,0:T(8,128)(2,1)S(1)}, bf16[8,640,128]{2,1,0:T(8,128)(2,1)S(1)}, u32[]{:S(2)}, u32[]{:S(2)}) %collective-permute-start.28) | collective-permute-done | bytes 1310752 | tf_op jit(solution)/shard_map/ppermute | solution.py:345
  183.2 3.2 %shard_map.136 = (f32[512,2048]{1,0:T(8,128)}, f32[512,512]{1,0:T(8,128)}) custom-call(s32[1]{0:T(128)} %bitcast.64.core_ref, bf16[8,640,128]{2,1,0:T(8,128)(2,1)S(1)} %shard_map.135.mine_ref, bf16[8,640,128]{2,1,0:T(8,128)(2,1)S(1)} %collective-permute-done.28.other_ref), custom_call_target="tpu_custom_call" | custom-call | tf_op jit(solution)/shard_map/pallas_call | solution.py:347
  (128 shorter events, 2.8 us)
Async XLA Ops:
  0.6 43.7 %collective-permute-start = (bf16[256,512]{1,0:T(8,128)(2,1)}, bf16[256,512]{1,0:T(8,128)(2,1)S(1)}, u32[]{:S(2)}, u32[]{:S(2)}) collective-permute-start(bf16[256,512]{1,0:T(8,128)(2,1)} %og_ref.1), channel_id=1, source_target_pairs={{0,1},{1,0},{2,3},{3,2},{4,5},{5,4},{6,7},{7,6},{8,9},{9,8},{10,11... | collective-permute-start | bytes 786440 | tf_op jit(solution)/shard_map/ppermute | solution.py:328
  3.2 1.0 copy-start
  4.2 1.0 copy-start.6
  5.2 0.9 copy-start.9
  8.1 4.6 %copy-start.17 = (s32[256]{0:T(256)S(1)}, s32[256]{0:T(256)}, u32[]{:S(2)}) copy-start(s32[256]{0:T(256)} %param.17) | copy-start | bytes 3076
  8.1 4.6 %copy-start.18 = (s32[256]{0:T(256)S(1)}, s32[256]{0:T(256)}, u32[]{:S(2)}) copy-start(s32[256]{0:T(256)} %param.19) | copy-start | bytes 3076
  8.1 4.7 %copy-start.14 = (s32[256]{0:T(256)S(1)}, s32[256]{0:T(256)}, u32[]{:S(2)}) copy-start(s32[256]{0:T(256)} %param.18) | copy-start | bytes 3076
  8.1 4.7 %copy-start.15 = (s32[256]{0:T(256)S(1)}, s32[256]{0:T(256)}, u32[]{:S(2)}) copy-start(s32[256]{0:T(256)} %param.16) | copy-start | bytes 3076
  8.1 6.7 %copy-start.10 = (s32[1,4]{1,0:T(1,128)S(1)}, s32[1,4]{1,0:T(1,128)}, u32[]{:S(2)}) copy-start(s32[1,4]{1,0:T(1,128)} %param.14) | copy-start | bytes 52
  8.1 7.3 %copy-start.16 = (s32[16,16]{1,0:T(8,128)S(1)}, s32[16,16]{1,0:T(8,128)}, u32[]{:S(2)}) copy-start(s32[16,16]{1,0:T(8,128)} %param.15) | copy-start | bytes 3076
  8.1 7.6 %copy-start.11 = (bf16[512,2048]{1,0:T(8,128)(2,1)S(1)}, bf16[512,2048]{1,0:T(8,128)(2,1)}, u32[]{:S(2)}) copy-start(bf16[512,2048]{1,0:T(8,128)(2,1)} %w_ref.1) | copy-start | bytes 6291460
  8.2 36.2 %all-to-all-start = ((bf16[8,288,512]{2,1,0:T(8,128)(2,1)}), bf16[8,288,512]{2,1,0:T(8,128)(2,1)}, u32[]{:S(2)}, u32[]{:S(2)}) async-start(bf16[8,288,512]{2,1,0:T(8,128)(2,1)} %shard_map.129), calls=%async_computation | async-start | bytes 4718592 | tf_op jit(solution)/shard_map/all_to_all | solution.py:398
  13.8 8.4 %collective-permute-start.1 = (s32[4,4,32]{2,1,0:T(4,128)S(1)}, s32[4,4,32]{2,1,0:T(4,128)S(1)}, u32[]{:S(2)}, u32[]{:S(2)}) collective-permute-start(s32[4,4,32]{2,1,0:T(4,128)S(1)} %bitcast.167), channel_id=1, source_target_pairs={{0,8},{8,0},{16,24},{24,16},{32,40},{40,32},{48,56},{56,48},{64,72... | collective-permute-start | bytes 6152 | tf_op jit(solution)/shard_map/ppermute | solution.py:304
  21.2 40.5 %copy-start.1 = (bf16[256,512]{1,0:T(8,128)(2,1)S(1)}, bf16[256,512]{1,0:T(8,128)(2,1)}, u32[]{:S(2)}) copy-start(bf16[256,512]{1,0:T(8,128)(2,1)} %og_ref.1) | copy-start | bytes 786436
  22.3 6.9 %collective-permute-start.4 = (s32[2,4,32]{2,1,0:T(4,128)S(1)}, s32[2,4,32]{2,1,0:T(4,128)S(1)}, u32[]{:S(2)}, u32[]{:S(2)}) collective-permute-start(s32[2,4,32]{2,1,0:T(4,128)S(1)} %get-tuple-element.89), channel_id=1, source_target_pairs={{0,64},{8,72},{16,80},{24,88},{32,96},{40,104},{48,112},{56,120},{... | collective-permute-start | bytes 3080 | tf_op jit(solution)/shard_map/ppermute | solution.py:304
  23.7 5.5 %collective-permute-start.3 = (s32[2,4,32]{2,1,0:T(4,128)S(1)}, s32[2,4,32]{2,1,0:T(4,128)S(1)}, u32[]{:S(2)}, u32[]{:S(2)}) collective-permute-start(s32[2,4,32]{2,1,0:T(4,128)S(1)} %get-tuple-element.90), channel_id=1, source_target_pairs={{0,128},{8,136},{16,144},{24,152},{32,160},{40,168},{48,176},{56,1... | collective-permute-start | bytes 3080 | tf_op jit(solution)/shard_map/ppermute | solution.py:304
  26.3 2.9 %collective-permute-start.2 = (s32[2,4,32]{2,1,0:T(4,128)S(1)}, s32[2,4,32]{2,1,0:T(4,128)S(1)}, u32[]{:S(2)}, u32[]{:S(2)}) collective-permute-start(s32[2,4,32]{2,1,0:T(4,128)S(1)} %get-tuple-element.91), channel_id=1, source_target_pairs={{0,192},{8,200},{16,208},{24,216},{32,224},{40,232},{48,240},{56,2... | collective-permute-start | bytes 3080 | tf_op jit(solution)/shard_map/ppermute | solution.py:304
  29.3 14.9 %collective-permute-start.6 = (s32[4,2,32]{2,1,0:T(2,128)S(1)}, s32[4,2,32]{2,1,0:T(2,128)S(1)}, u32[]{:S(2)}, u32[]{:S(2)}) collective-permute-start(s32[4,2,32]{2,1,0:T(2,128)S(1)} %bitcast.170), channel_id=1, source_target_pairs={{0,32},{8,40},{16,48},{24,56},{32,0},{40,8},{48,16},{56,24},{64,96... | collective-permute-start | bytes 3080 | tf_op jit(solution)/shard_map/ppermute | solution.py:304
  35.7 8.5 %collective-permute-start.7 = (s32[4,2,32]{2,1,0:T(2,128)S(1)}, s32[4,2,32]{2,1,0:T(2,128)S(1)}, u32[]{:S(2)}, u32[]{:S(2)}) collective-permute-start(s32[4,2,32]{2,1,0:T(2,128)S(1)} %bitcast.169), channel_id=1, source_target_pairs={{0,16},{8,24},{16,32},{24,40},{32,48},{40,56},{48,0},{56,8},{64,80... | collective-permute-start | bytes 3080 | tf_op jit(solution)/shard_map/ppermute | solution.py:304
  36.9 3.8 %collective-permute-start.5 = (s32[4,2,32]{2,1,0:T(2,128)S(1)}, s32[4,2,32]{2,1,0:T(2,128)S(1)}, u32[]{:S(2)}, u32[]{:S(2)}) collective-permute-start(s32[4,2,32]{2,1,0:T(2,128)S(1)} %bitcast.171), channel_id=1, source_target_pairs={{0,48},{8,56},{16,0},{24,8},{32,16},{40,24},{48,32},{56,40},{64,11... | collective-permute-start | bytes 3080 | tf_op jit(solution)/shard_map/ppermute | solution.py:304
  44.3 0.7 copy-start.12
  45.0 16.7 %copy-start.13 = (bf16[256,512]{1,0:T(8,128)(2,1)S(1)}, bf16[256,512]{1,0:T(8,128)(2,1)}, u32[]{:S(2)}) copy-start(bf16[256,512]{1,0:T(8,128)(2,1)} %copy-done.12) | copy-start | bytes 786436
  55.7 0.8 copy-start.4
  56.5 11.6 %all-to-all-start.1 = ((f32[8,4,2048]{2,1,0:T(4,128)}), f32[8,4,2048]{2,1,0:T(4,128)S(1)}, u32[]{:S(2)}, u32[]{:S(2)}) async-start(f32[8,4,2048]{2,1,0:T(4,128)} %get-tuple-element.46), calls=%async_computation.1 | async-start | bytes 524288 | tf_op jit(solution)/shard_map/all_to_all | solution.py:433
  61.7 20.7 %collective-permute-start.9 = (bf16[2,256,512]{2,1,0:T(8,128)(2,1)S(1)}, bf16[2,256,512]{2,1,0:T(8,128)(2,1)S(1)}, u32[]{:S(2)}, u32[]{:S(2)}) collective-permute-start(bf16[2,256,512]{2,1,0:T(8,128)(2,1)S(1)} %pad_maximum_fusion.refs_0_), channel_id=1, source_target_pairs={{0,4},{1,5},{2,6},{3,7},{4,0},{5,1},{6,2},{7,3},{8,12},{9,13},{10,... | collective-permute-start | bytes 1572872 | tf_op jit(solution)/shard_map/ppermute | solution.py:328
  68.1 22.4 %collective-permute-start.10 = (bf16[2,256,512]{2,1,0:T(8,128)(2,1)S(1)}, bf16[2,256,512]{2,1,0:T(8,128)(2,1)S(1)}, u32[]{:S(2)}, u32[]{:S(2)}) collective-permute-start(bf16[2,256,512]{2,1,0:T(8,128)(2,1)S(1)} %pad_maximum_fusion.refs_0_), channel_id=1, source_target_pairs={{0,6},{1,7},{2,4},{3,5},{4,2},{5,3},{6,0},{7,1},{8,14},{9,15},{10,... | collective-permute-start | bytes 1572872 | tf_op jit(solution)/shard_map/ppermute | solution.py:328
  68.4 22.9 %collective-permute-start.8 = (bf16[2,256,512]{2,1,0:T(8,128)(2,1)S(1)}, bf16[2,256,512]{2,1,0:T(8,128)(2,1)}, u32[]{:S(2)}, u32[]{:S(2)}) collective-permute-start(bf16[2,256,512]{2,1,0:T(8,128)(2,1)S(1)} %pad_maximum_fusion.refs_0_), channel_id=1, source_target_pairs={{0,2},{1,3},{2,0},{3,1},{4,6},{5,7},{6,4},{7,5},{8,10},{9,11},{10,... | collective-permute-start | bytes 1572872 | tf_op jit(solution)/shard_map/ppermute | solution.py:328
  68.9 1.0 copy-start.5
  81.8 0.7 copy-start.7
  82.5 12.5 %copy-start.8 = (bf16[64,2048]{1,0:T(8,128)(2,1)S(1)}, bf16[64,2048]{1,0:T(8,128)(2,1)}, u32[]{:S(2)}) copy-start(bf16[64,2048]{1,0:T(8,128)(2,1)} %copy-done.7) | copy-start | bytes 786436
  90.5 0.8 copy-start.2
  91.3 3.7 %copy-start.3 = (bf16[2,256,512]{2,1,0:T(8,128)(2,1)S(1)}, bf16[2,256,512]{2,1,0:T(8,128)(2,1)}, u32[]{:S(2)}) copy-start(bf16[2,256,512]{2,1,0:T(8,128)(2,1)} %copy-done.2) | copy-start | bytes 1572868
  91.3 23.0 %all-to-all-start.2 = ((bf16[8,272,256]{2,1,0:T(8,128)(2,1)}), bf16[8,272,256]{2,1,0:T(8,128)(2,1)S(1)}, u32[]{:S(2)}, u32[]{:S(2)}) async-start(bf16[8,272,256]{2,1,0:T(8,128)(2,1)} %get-tuple-element.55.gp_ref), calls=%async_computation.2 | async-start | bytes 2228224 | tf_op jit(solution)/shard_map/all_to_all | solution.py:452
  98.3 7.0 %collective-permute-start.11 = (f32[640,128]{1,0:T(8,128)S(1)}, f32[640,128]{1,0:T(8,128)S(1)}, u32[]{:S(2)}, u32[]{:S(2)}) collective-permute-start(f32[640,128]{1,0:T(8,128)S(1)} %dynamic-slice_bitcast_fusion), channel_id=1, source_target_pairs={{0,8},{8,0},{16,24},{24,16},{32,40},{40,32},{48,56},{56,48},{64,72... | collective-permute-start | bytes 983048 | tf_op jit(solution)/shard_map/ppermute | solution.py:340
  105.4 6.4 %collective-permute-start.12 = (f32[160,128]{1,0:T(8,128)S(1)}, f32[160,128]{1,0:T(8,128)S(1)}, u32[]{:S(2)}, u32[]{:S(2)}) collective-permute-start(f32[160,128]{1,0:T(8,128)S(1)} %get-tuple-element.78), channel_id=1, source_target_pairs={{0,64},{8,72},{16,80},{24,88},{32,96},{40,104},{48,112},{56,120},{... | collective-permute-start | bytes 245768 | tf_op jit(solution)/shard_map/ppermute | solution.py:291
  106.1 6.1 %collective-permute-start.14 = (f32[160,128]{1,0:T(8,128)S(1)}, f32[160,128]{1,0:T(8,128)S(1)}, u32[]{:S(2)}, u32[]{:S(2)}) collective-permute-start(f32[160,128]{1,0:T(8,128)S(1)} %get-tuple-element.79), channel_id=1, source_target_pairs={{0,192},{8,200},{16,208},{24,216},{32,224},{40,232},{48,240},{56,2... | collective-permute-start | bytes 245768 | tf_op jit(solution)/shard_map/ppermute | solution.py:291
  108.2 6.1 %collective-permute-start.13 = (f32[160,128]{1,0:T(8,128)S(1)}, f32[160,128]{1,0:T(8,128)S(1)}, u32[]{:S(2)}, u32[]{:S(2)}) collective-permute-start(f32[160,128]{1,0:T(8,128)S(1)} %get-tuple-element.80), channel_id=1, source_target_pairs={{0,128},{8,136},{16,144},{24,152},{32,160},{40,168},{48,176},{56,1... | collective-permute-start | bytes 245768 | tf_op jit(solution)/shard_map/ppermute | solution.py:291
  114.3 8.8 %collective-permute-start.17 = (f32[160,128]{1,0:T(8,128)S(1)}, f32[160,128]{1,0:T(8,128)S(1)}, u32[]{:S(2)}, u32[]{:S(2)}) collective-permute-start(f32[160,128]{1,0:T(8,128)S(1)} %fusion.3), channel_id=1, source_target_pairs={{0,48},{8,56},{16,0},{24,8},{32,16},{40,24},{48,32},{56,40},{64,11... | collective-permute-start | bytes 245768 | tf_op jit(solution)/shard_map/ppermute | solution.py:296
  114.4 8.7 %collective-permute-start.16 = (f32[160,128]{1,0:T(8,128)S(1)}, f32[160,128]{1,0:T(8,128)S(1)}, u32[]{:S(2)}, u32[]{:S(2)}) collective-permute-start(f32[160,128]{1,0:T(8,128)S(1)} %fusion.3), channel_id=1, source_target_pairs={{0,32},{8,40},{16,48},{24,56},{32,0},{40,8},{48,16},{56,24},{64,96... | collective-permute-start | bytes 245768 | tf_op jit(solution)/shard_map/ppermute | solution.py:296
  117.5 7.4 %collective-permute-start.15 = (f32[160,128]{1,0:T(8,128)S(1)}, f32[160,128]{1,0:T(8,128)S(1)}, u32[]{:S(2)}, u32[]{:S(2)}) collective-permute-start(f32[160,128]{1,0:T(8,128)S(1)} %fusion.3), channel_id=1, source_target_pairs={{0,16},{8,24},{16,32},{24,40},{32,48},{40,56},{48,0},{56,8},{64,80... | collective-permute-start | bytes 245768 | tf_op jit(solution)/shard_map/ppermute | solution.py:296
  124.9 16.3 %collective-permute-start.20 = (bf16[160,128]{1,0:T(8,128)(2,1)S(1)}, bf16[160,128]{1,0:T(8,128)(2,1)S(1)}, u32[]{:S(2)}, u32[]{:S(2)}) collective-permute-start(bf16[160,128]{1,0:T(8,128)(2,1)S(1)} %add_add_fusion), channel_id=1, source_target_pairs={{0,64},{8,72},{16,80},{24,88},{32,96},{40,104},{48,112},{56,120},{... | collective-permute-start | bytes 122888 | tf_op jit(solution)/shard_map/ppermute | solution.py:304
  125.0 16.1 %collective-permute-start.19 = (bf16[160,128]{1,0:T(8,128)(2,1)S(1)}, bf16[160,128]{1,0:T(8,128)(2,1)S(1)}, u32[]{:S(2)}, u32[]{:S(2)}) collective-permute-start(bf16[160,128]{1,0:T(8,128)(2,1)S(1)} %add_add_fusion), channel_id=1, source_target_pairs={{0,128},{8,136},{16,144},{24,152},{32,160},{40,168},{48,176},{56,1... | collective-permute-start | bytes 122888 | tf_op jit(solution)/shard_map/ppermute | solution.py:304
  129.2 11.9 %collective-permute-start.18 = (bf16[160,128]{1,0:T(8,128)(2,1)S(1)}, bf16[160,128]{1,0:T(8,128)(2,1)S(1)}, u32[]{:S(2)}, u32[]{:S(2)}) collective-permute-start(bf16[160,128]{1,0:T(8,128)(2,1)S(1)} %add_add_fusion), channel_id=1, source_target_pairs={{0,192},{8,200},{16,208},{24,216},{32,224},{40,232},{48,240},{56,2... | collective-permute-start | bytes 122888 | tf_op jit(solution)/shard_map/ppermute | solution.py:304
  129.2 44.3 %all-to-all-start.3 = ((bf16[256,16,128]{2,1,0:T(8,128)(2,1)}), bf16[256,16,128]{2,1,0:T(8,128)(2,1)S(1)}, u32[]{:S(2)}, u32[]{:S(2)}) async-start(bf16[256,16,128]{2,1,0:T(8,128)(2,1)} %shard_map.133), calls=%async_computation.3 | async-start | bytes 2097152 | tf_op jit(solution)/shard_map/all_to_all | solution.py:469
  141.3 28.9 %collective-permute-start.27 = (bf16[640,128]{1,0:T(8,128)(2,1)S(1)}, bf16[640,128]{1,0:T(8,128)(2,1)S(1)}, u32[]{:S(2)}, u32[]{:S(2)}) collective-permute-start(bf16[640,128]{1,0:T(8,128)(2,1)S(1)} %bitcast.142), channel_id=1, source_target_pairs={{0,7},{1,6},{2,5},{3,4},{4,3},{5,2},{6,1},{7,0},{8,15},{9,14},{10,... | collective-permute-start | bytes 491528 | tf_op jit(solution)/shard_map/ppermute | solution.py:328
  145.0 25.2 %collective-permute-start.26 = (bf16[640,128]{1,0:T(8,128)(2,1)S(1)}, bf16[640,128]{1,0:T(8,128)(2,1)S(1)}, u32[]{:S(2)}, u32[]{:S(2)}) collective-permute-start(bf16[640,128]{1,0:T(8,128)(2,1)S(1)} %bitcast.143), channel_id=1, source_target_pairs={{0,6},{1,7},{2,4},{3,5},{4,2},{5,3},{6,0},{7,1},{8,14},{9,15},{10,... | collective-permute-start | bytes 491528 | tf_op jit(solution)/shard_map/ppermute | solution.py:328
  145.5 30.2 %collective-permute-start.25 = (bf16[640,128]{1,0:T(8,128)(2,1)S(1)}, bf16[640,128]{1,0:T(8,128)(2,1)S(1)}, u32[]{:S(2)}, u32[]{:S(2)}) collective-permute-start(bf16[640,128]{1,0:T(8,128)(2,1)S(1)} %bitcast.144), channel_id=1, source_target_pairs={{0,5},{1,4},{2,7},{3,6},{4,1},{5,0},{6,3},{7,2},{8,13},{9,12},{10,... | collective-permute-start | bytes 491528 | tf_op jit(solution)/shard_map/ppermute | solution.py:328
  146.9 28.8 %collective-permute-start.24 = (bf16[640,128]{1,0:T(8,128)(2,1)S(1)}, bf16[640,128]{1,0:T(8,128)(2,1)S(1)}, u32[]{:S(2)}, u32[]{:S(2)}) collective-permute-start(bf16[640,128]{1,0:T(8,128)(2,1)S(1)} %bitcast.145), channel_id=1, source_target_pairs={{0,4},{1,5},{2,6},{3,7},{4,0},{5,1},{6,2},{7,3},{8,12},{9,13},{10,... | collective-permute-start | bytes 491528 | tf_op jit(solution)/shard_map/ppermute | solution.py:328
  148.4 27.6 %collective-permute-start.23 = (bf16[640,128]{1,0:T(8,128)(2,1)S(1)}, bf16[640,128]{1,0:T(8,128)(2,1)S(1)}, u32[]{:S(2)}, u32[]{:S(2)}) collective-permute-start(bf16[640,128]{1,0:T(8,128)(2,1)S(1)} %bitcast.146), channel_id=1, source_target_pairs={{0,3},{1,2},{2,1},{3,0},{4,7},{5,6},{6,5},{7,4},{8,11},{9,10},{10,... | collective-permute-start | bytes 491528 | tf_op jit(solution)/shard_map/ppermute | solution.py:328
  170.2 9.6 %collective-permute-start.22 = (bf16[640,128]{1,0:T(8,128)(2,1)S(1)}, bf16[640,128]{1,0:T(8,128)(2,1)S(1)}, u32[]{:S(2)}, u32[]{:S(2)}) collective-permute-start(bf16[640,128]{1,0:T(8,128)(2,1)S(1)} %bitcast.147), channel_id=1, source_target_pairs={{0,2},{1,3},{2,0},{3,1},{4,6},{5,7},{6,4},{7,5},{8,10},{9,11},{10,... | collective-permute-start | bytes 491528 | tf_op jit(solution)/shard_map/ppermute | solution.py:328
  170.2 9.6 %collective-permute-start.21 = (bf16[640,128]{1,0:T(8,128)(2,1)S(1)}, bf16[640,128]{1,0:T(8,128)(2,1)S(1)}, u32[]{:S(2)}, u32[]{:S(2)}) collective-permute-start(bf16[640,128]{1,0:T(8,128)(2,1)S(1)} %bitcast.148), channel_id=1, source_target_pairs={{0,1},{1,0},{2,3},{3,2},{4,5},{5,4},{6,7},{7,6},{8,9},{9,8},{10,11... | collective-permute-start | bytes 491528 | tf_op jit(solution)/shard_map/ppermute | solution.py:328
  179.9 3.2 %collective-permute-start.28 = (bf16[8,640,128]{2,1,0:T(8,128)(2,1)S(1)}, bf16[8,640,128]{2,1,0:T(8,128)(2,1)S(1)}, u32[]{:S(2)}, u32[]{:S(2)}) collective-permute-start(bf16[8,640,128]{2,1,0:T(8,128)(2,1)S(1)} %shard_map.135.mine_ref), channel_id=1, source_target_pairs={{0,8},{8,0},{16,24},{24,16},{32,40},{40,32},{48,56},{56,48},{64,72... | collective-permute-start | bytes 3932168 | tf_op jit(solution)/shard_map/ppermute | solution.py:345
where the time goes:
time: 188 us; the launch traced here: 186 us
  starting transfers between devices  76.5 us (41%)
  waiting for transfers between devices  53.8 us (29%)
  Pallas kernels  37.7 us (20%)
  local copies, waits for them, and re-layouts  13.3 us (7%)
  between operations  3.4 us (2%)
    ppermute x11, waiting for transfers between devices, over_ctx(): return lax.ppermute(x, 'ctx', [(i, i ^ k) for i in range(8)])  32.8 us
    ppermute x10, starting transfers between devices, by_source(): held.append(lax.ppermute(sent, 'dp', turned(stride, size, k)))  20.4 us
    ppermute x11, starting transfers between devices, over_ctx(): return lax.ppermute(x, 'ctx', [(i, i ^ k) for i in range(8)])  13.9 us
    all_to_all x1, starting transfers between devices, body(): arrived = lax.all_to_all(packed, ('dp', 'ctx'), 0, 0, tiled=True)  11.9 us
    pallas_call x1, Pallas kernels, body(): call(backward_kernel, (out((NB, 4 * HD + 16, TOK), BF), out((HD, LEN), BF...  11.8 us
    pallas_call x1, Pallas kernels, body(): call(forward_kernel, (out((4 * HD, LEN), BF), out((4 * HD, LEN), F32), ou...  10.7 us
    unnamed x64, local copies, waits for them, and re-layouts  9.75 us
    ppermute x10, waiting for transfers between devices, by_source(): held.append(lax.ppermute(sent, 'dp', turned(stride, size, k)))  6.73 us
  transfers between devices with their start and end apart: 33, of which 14 were waited for; matrix products, arithmetic and copies ran while one was open for 4% of the time, Pallas kernels for 13%

commit v1 on v0

--- a/solution.py
+++ b/solution.py
@@ -13,6 +13,8 @@
 LEN = 2048
 NT = 16
 NB = 8
+QB = 512
+QN = 4
 LMAX = 1024
 CAP = 2
 DEVICES = 256
@@ -21,6 +23,7 @@
 BF = jnp.bfloat16
 F32 = jnp.float32
 MEMORY = 50 * 1024 * 1024
+SMALL = 24 * 1024 * 1024
 
 NN = (((1,), (0,)), ((), ()))
 NT_DIMS = (((1,), (1,)), ((), ()))
@@ -30,7 +33,7 @@
     return lax.dot_general(a, b, dims, preferred_element_type=F32)
 
 
-def call(kernel, outs, scratch=(), smem=0, n_in=0):
+def call(kernel, outs, scratch=(), smem=0, n_in=0, memory=MEMORY):
     specs = [pl.BlockSpec(memory_space=pltpu.SMEM)] * smem + [
         pl.BlockSpec(memory_space=pltpu.VMEM)
     ] * (n_in - smem)
@@ -40,7 +43,7 @@
         in_specs=specs,
         out_specs=jax.tree.map(lambda _: pl.BlockSpec(memory_space=pltpu.VMEM), outs),
         scratch_shapes=list(scratch),
-        compiler_params=pltpu.CompilerParams(vmem_limit_bytes=MEMORY),
+        compiler_params=pltpu.CompilerParams(vmem_limit_bytes=memory),
     )
 
 
@@ -78,12 +81,12 @@
 def seen(lo_ref, kb, k0, qs, row_pos):
     lower = jnp.concatenate(
         [
-            jnp.broadcast_to(lo_ref[2 * kb, :, qs], (TILE, TOK)),
-            jnp.broadcast_to(lo_ref[2 * kb + 1, :, qs], (TILE, TOK)),
+            jnp.broadcast_to(lo_ref[2 * kb, :, qs], (TILE, QB)),
+            jnp.broadcast_to(lo_ref[2 * kb + 1, :, qs], (TILE, QB)),
         ],
         axis=0,
     )
-    col_pos = k0 + lax.broadcasted_iota(jnp.int32, (TOK, TOK), 0)
+    col_pos = k0 + lax.broadcasted_iota(jnp.int32, (TOK, QB), 0)
     return (col_pos >= lower) & (col_pos <= row_pos)
 
 
@@ -101,10 +104,10 @@
         act_ref[:, cs] = a
         ds_ref[:, cs] = (0.5 * (1.0 + t)) * (1.0 + (h - u))
         k_s[cs, :] = a[2 * HD : 3 * HD].T
-    for qb in range(NB):
-        qs = pl.ds(qb * TOK, TOK)
+    for qb in range(QN):
+        qs = pl.ds(qb * QB, QB)
         qt = act_ref[:HD, qs] * BF(0.0625)
-        row_pos = qb * TOK + lax.broadcasted_iota(jnp.int32, (1, TOK), 1)
+        row_pos = qb * QB + lax.broadcasted_iota(jnp.int32, (1, QB), 1)
 
         def step(kb, acc):
             k0 = pl.multiple_of(kb * TOK, TOK)
@@ -114,13 +117,13 @@
             return acc + mm(act_ref[HD : 2 * HD, pl.ds(k0, TOK)], a)
 
         acc = lax.fori_loop(
-            first_event(len_ref, qb * TOK) // TOK, qb + 1, step, jnp.zeros((HD, TOK), F32)
+            first_event(len_ref, qb * QB) // TOK, (qb + 1) * (QB // TOK), step, jnp.zeros((HD, QB), F32)
         )
         m = acc * (1.0 / LMAX)
         mix_ref[:, qs] = m
         s1 = jnp.sum(m, axis=0, keepdims=True)
         c = m - s1 * (1.0 / HD)
-        gn = gate_cotangent(r_ref, qb) * act_ref[3 * HD :, qs].astype(F32)
+        gn = jnp.concatenate([gate_cotangent(r_ref, s) for s in range(qb * QB // TOK, (qb + 1) * QB // TOK)], axis=1) * act_ref[3 * HD :, qs].astype(F32)
         st_ref[0:1, qs] = s1
         st_ref[1:2, qs] = jnp.sum(c * c, axis=0, keepdims=True)
         st_ref[2:3, qs] = jnp.sum(gn, axis=0, keepdims=True)
@@ -153,11 +156,11 @@
         gated_ref[:, cs] = (normed * gate).astype(BF)
         dm_s[:, cs] = (inv * (gg * gate - mean_gn - normed * mean_gnn)).astype(BF)
         gp_ref[s, 3 * HD : 4 * HD, :] = (gg * normed * ds_ref[3 * HD :, cs]).astype(BF)
-    for qb in range(NB):
-        qs = pl.ds(qb * TOK, TOK)
+    for qb in range(QN):
+        qs = pl.ds(qb * QB, QB)
         qt = act_ref[:HD, qs] * BF(0.0625)
         dm = dm_s[:, qs]
-        row_pos = qb * TOK + lax.broadcasted_iota(jnp.int32, (1, TOK), 1)
+        row_pos = qb * QB + lax.broadcasted_iota(jnp.int32, (1, QB), 1)
 
         def step(kb, acc):
             k0 = pl.multiple_of(kb * TOK, TOK)
@@ -174,9 +177,11 @@
             return acc + mm(act_ref[2 * HD : 3 * HD, ks], d)
 
         acc = lax.fori_loop(
-            first_event(len_ref, qb * TOK) // TOK, qb + 1, step, jnp.zeros((HD, TOK), F32)
+            first_event(len_ref, qb * QB) // TOK, (qb + 1) * (QB // TOK), step, jnp.zeros((HD, QB), F32)
         )
-        gp_ref[qb, :HD, :] = (acc * (1.0 / (16 * LMAX)) * ds_ref[:HD, qs]).astype(BF)
+        dq = (acc * (1.0 / (16 * LMAX)) * ds_ref[:HD, qs]).astype(BF)
+        for i in range(QB // TOK):
+            gp_ref[qb * (QB // TOK) + i, :HD, :] = dq[:, i * TOK : (i + 1) * TOK]
     for s in range(NB):
         cs = pl.ds(s * TOK, TOK)
         gp_ref[s, HD : 2 * HD, :] = (dv_s[:, cs] * (1.0 / LMAX) * ds_ref[HD : 2 * HD, cs]).astype(BF)
@@ -184,13 +189,14 @@
 
 
 def weight_kernel(place_ref, gp_ref, r_ref, gated_ref, *refs):
-    ch_ref = refs[NB // 2]
+    pair_ref, a_ref, far_a_ref, far_b_ref, b_ref, ch_ref = refs
+    blocks = [pair_ref.at[0], pair_ref.at[1], a_ref.at[0], a_ref.at[1], far_a_ref, far_b_ref, b_ref.at[0], b_ref.at[1]]
     pw = jnp.zeros((4 * HD, D), F32)
     ow = jnp.zeros((HD, D), F32)
     for s in range(NB):
         pw = pw + mm(gp_ref[s, : 4 * HD], r_ref[s, :TOK, :])
         first = pl.multiple_of((place_ref[0] ^ s) * TOK, TOK)
-        ow = ow + mm(gated_ref[:, pl.ds(first, TOK)], refs[s // 2][s % 2])
+        ow = ow + mm(gated_ref[:, pl.ds(first, TOK)], blocks[s][...])
     pw = pw.T
     ch_ref[:D, :] = pw[:, :128]
     ch_ref[D : 2 * D, :] = pw[:, 128:]
@@ -230,9 +236,16 @@
         o_ref[...] = mm(same, rows)
 
 
-def place_kernel(place_ref, *refs):
-    for k in range(HEADS):
-        refs[HEADS][place_ref[0] ^ k] = refs[k][...]
+def place_kernel(place_ref, y_ref, *refs):
+    own_ref, a_ref, far_a_ref, far_b_ref, b_ref, out_ref = refs
+    for j in range(4):
+        first = pl.multiple_of((y_ref[0] ^ j) * 160, 32)
+        for k in range(HEADS):
+            if j == 2:
+                piece = far_a_ref[k] if k < 4 else far_b_ref[k - 4]
+            else:
+                piece = (own_ref, a_ref, None, b_ref)[j][k]
+            out_ref[place_ref[0] ^ k, pl.ds(first, 160), :] = piece
 
 
 def weights_out_kernel(core_ref, mine_ref, other_ref, pw_ref, ow_ref):
@@ -292,36 +305,42 @@
     return total
 
 
-def total(x, stride):
-    return x + sum(lax.ppermute(x, "dp", turned(stride, 4, k)) for k in (1, 2, 3))
-
-
-def by_source(parts, stride, size):
+def over_z(x):
+    return [lax.ppermute(x, "dp", turned(2, 4, k)) for k in (1, 2, 3)]
+
+
+def to_source(parts, stride, size):
     me = (lax.axis_index("dp") // stride) % size
     held = [lax.dynamic_index_in_dim(parts, me, 0, False)]
     for k in range(1, size):
         sent = lax.dynamic_index_in_dim(parts, (me + k) % size, 0, False)
         held.append(lax.ppermute(sent, "dp", turned(stride, size, k)))
+    return held
+
+
+def by_source(held, stride):
+    size = len(held)
+    me = (lax.axis_index("dp") // stride) % size
     back = jnp.stack([held[-i % size] for i in range(size)] * 2)
     return lax.dynamic_slice_in_dim(back, (size - me) % size, size, 0)
 
 
-def gathered(x, stride):
-    return by_source(jnp.broadcast_to(x[None], (4,) + x.shape), stride, 4).reshape(-1, 128)
-
-
 def labels_over_dp(labels):
     x = labels.reshape(4, 4, 2, 32)
-    x = by_source(x.transpose(2, 0, 1, 3), 1, 2)
-    x = by_source(x.transpose(1, 0, 2, 3), 8, 4)
-    x = by_source(x.transpose(2, 0, 1, 3), 2, 4)
-    return x.transpose(1, 0, 2, 3)
-
-
-def label_digits(x):
+    x = by_source(to_source(x.transpose(2, 0, 1, 3), 1, 2), 1)
+    x = by_source(to_source(x.transpose(1, 0, 2, 3), 8, 4), 8)
+    return to_source(x.transpose(2, 0, 1, 3), 2, 4)
+
+
+def label_digits(held):
+    x = by_source(held, 2).transpose(1, 0, 2, 3)
     x = x.reshape(32, 8, 4).transpose(1, 0, 2).reshape(8, 128)
     x = jnp.concatenate([(x + 1) // 256, (x + 1) % 256], axis=1)
     return jnp.broadcast_to(x[:, None], (8, 16, 256)).astype(BF)
+
+
+def over_y(x, k):
+    return lax.ppermute(x, "dp", [(i, i ^ (8 * k)) for i in range(32)])
 
 
 def over_ctx(x, k):
@@ -420,7 +439,7 @@
     beside = over_ctx(out_grad, 1)
     received, beside = together(received, beside)
     grad_pair = jnp.stack([out_grad, beside])
-    far_pair = over_ctx(grad_pair, 4)
+    near_a, near_b = over_ctx(grad_pair, 2), over_ctx(grad_pair, 6)
 
     act, slope, mixed, stats = call(
         forward_kernel,
@@ -429,11 +448,11 @@
         smem=1,
         n_in=4,
     )(history, received, own_t, lower)
-    stats, labels = together(stats, labels)
+    stats, *labels = together(stats, *labels)
     all_stats = lax.all_to_all(stats, "ctx", 0, 0, tiled=True)
     labels = label_digits(labels)
-    all_stats, grad_pair = together(all_stats, grad_pair)
-    group_grad = [grad_pair, over_ctx(grad_pair, 2), far_pair, over_ctx(grad_pair, 6)]
+    all_stats, near_a, near_b = together(all_stats, near_a, near_b)
+    group_grad = [grad_pair, near_a, over_ctx(near_a[0], 6), over_ctx(near_b[1], 2), near_b]
     grads, gated = call(
         backward_kernel,
         (out((NB, 4 * HD + 16, TOK), BF), out((HD, LEN), BF)),
@@ -453,21 +472,26 @@
     marks = back[:, 4 * HD].astype(F32).astype(jnp.int32)
     marks = marks[:, :128] * 256 + marks[:, 128:] - 1
     marks = marks.reshape(8, 32, 4).transpose(1, 0, 2).reshape(DEVICES, 2, CAP)
-    terms = call(weight_kernel, out((1280, 128), F32), smem=1, n_in=8)(
+    terms = call(weight_kernel, out((1280, 128), F32), smem=1, n_in=9)(
         head.reshape(1).astype(jnp.int32), grads, received, gated, *group_grad
     )
     terms = scatter_sum(core_sum(terms), 8)
     back, terms = together(back, terms)
-    terms = total(terms, 2)
+    others = over_z(terms)
     packed = call(
         pack_kernel,
         out((DEVICES, 16, 128), BF),
         [pltpu.VMEM((4 * D, TOK), BF), pltpu.VMEM((DEVICES * 16, 128), F32)],
         n_in=5,
     )(back, proj_weight, out_grad, quotient_target.reshape(1, TOK), remainder_target.reshape(1, TOK))
+    packed, *others = together(packed, *others)
+    terms = (terms + sum(others)).astype(BF)
+    terms = jnp.stack([terms, over_ctx(terms, 1)])
     packed, terms = together(packed, terms)
     arrived = lax.all_to_all(packed, ("dp", "ctx"), 0, 0, tiled=True)
-    terms = gathered(terms, 8).astype(BF)
+    terms = jnp.concatenate([terms] + [over_ctx(terms, k) for k in (2, 4, 6)])
+    y_a, y_b = over_y(terms, 1), over_y(terms, 3)
+    held = [terms, y_a, over_y(y_a[:4], 3), over_y(y_b[4:], 1), y_b]
     columns = [marks[:, t].reshape(DEVICES * CAP, 1) for t in range(2)]
     rows = [marks[:, t].T.reshape(1, DEVICES * CAP) for t in range(2)]
     quotient_grads, remainder_grads = call(
@@ -476,9 +500,11 @@
         [pltpu.VMEM((DEVICES * 16, 128), F32)],
         n_in=5,
     )(arrived, columns[0], rows[0], columns[1], rows[1])
-    held = [terms] + [over_ctx(terms, k) for k in range(1, 8)]
     quotient_grads, *held = together(quotient_grads, *held)
-    terms = call(place_kernel, out((HEADS, 640, 128), BF), smem=1, n_in=9)(head.reshape(1).astype(jnp.int32), *held)
+    y_place = (lax.axis_index("dp") // 8).reshape(1).astype(jnp.int32)
+    terms = call(place_kernel, out((HEADS, 640, 128), BF), smem=2, n_in=7, memory=SMALL)(
+        head.reshape(1).astype(jnp.int32), y_place, *held
+    )
     proj_weight_grad, out_weight_grad = weights_out(terms)
     return (quotient_grads, remainder_grads, proj_weight_grad, out_weight_grad)
 

time: 188 us -> 177 us (0.941)
  waiting for transfers between devices: 53.8 us -> 45.6 us
  starting transfers between devices: 76.5 us -> 74 us
    ppermute x11 -> x9, waiting for transfers between devices: 32.8 us -> 8.43 us  [over_ctx(): return lax.ppermute(x, 'ctx', [(i, i ^ k) for i in range(8)])]
    ppermute x13 -> x14, waiting for transfers between devices: 8.59 us -> 14.4 us  [the longest x4 10.7 us: over_y(): return lax.ppermute(x, 'dp', [(i, i ^ 8 * k) for i in range(32)])]
    ppermute x11 -> x9, starting transfers between devices: 13.9 us -> 8.79 us  [over_ctx(): return lax.ppermute(x, 'ctx', [(i, i ^ k) for i in range(8)])]
    all_to_all x1, waiting for transfers between devices: 0.01 us -> 3.47 us  [body(): received = lax.all_to_all(sent, 'ctx', 0, 0, tiled=True)]
    all_to_all x1, waiting for transfers between devices: 2.71 us -> 5.75 us  [body(): arrived = lax.all_to_all(packed, ('dp', 'ctx'), 0, 0, tiled=True)]
    ppermute x3, starting transfers between devices: 6.35 us -> 3.5 us  [scatter_sum(): total = total + lax.ppermute(sent, 'dp', turned(stride, 4, k))]
    ppermute x1, starting transfers between devices: 5.76 us -> 8.34 us  [core_sum(): return mine + lax.ppermute(other, 'dp', turned(1, 2, 1))]
    all_to_all x1, waiting for transfers between devices: 3.31 us -> 5.59 us  [body(): all_stats = lax.all_to_all(stats, 'ctx', 0, 0, tiled=True)]
  transfers between devices with their start and end apart: 33 -> 32, of which waited for: 14 -> 15; matrix products, arithmetic and copies ran while one was open for 4% -> 4% of each run, Pallas kernels for 13% -> 20%
where the time goes in v1:
time: 177 us; the launch traced here: 175 us
  starting transfers between devices  74 us (42%)
  waiting for transfers between devices  45.6 us (26%)
  Pallas kernels  37.8 us (21%)
  local copies, waits for them, and re-layouts  13.1 us (7%)
  between operations  3.29 us (2%)
    ppermute x7, starting transfers between devices, to_source(): held.append(lax.ppermute(sent, 'dp', turned(stride, size, k)))  14.9 us
    all_to_all x1, starting transfers between devices, body(): arrived = lax.all_to_all(packed, ('dp', 'ctx'), 0, 0, tiled=True)  13.7 us
    pallas_call x1, Pallas kernels, body(): call(backward_kernel, (out((NB, 4 * HD + 16, TOK), BF), out((HD, LEN), BF...  12.8 us
    ppermute x4, waiting for transfers between devices, over_y(): return lax.ppermute(x, 'dp', [(i, i ^ 8 * k) for i in range(32)])  10.7 us
    pallas_call x1, Pallas kernels, body(): call(forward_kernel, (out((4 * HD, LEN), BF), out((4 * HD, LEN), F32), ou...  9.84 us
    unnamed x52, local copies, waits for them, and re-layouts  9.54 us
    ppermute x9, starting transfers between devices, over_ctx(): return lax.ppermute(x, 'ctx', [(i, i ^ k) for i in range(8)])  8.79 us
    ppermute x9, waiting for transfers between devices, over_ctx(): return lax.ppermute(x, 'ctx', [(i, i ^ k) for i in range(8)])  8.43 us
  transfers between devices with their start and end apart: 32, of which 15 were waited for; matrix products, arithmetic and copies ran while one was open for 4% of the time, Pallas kernels for 20%

profile of v1, /device:TPU:1, one launch (start us, length us, event | category | flops | bytes accessed | tf_op | source)
XLA Modules:
  0.0 175.3 jit_solution(173200467582169318)
XLA Ops:
  0.6 2.6 %collective-permute-start = (bf16[256,512]{1,0:T(8,128)(2,1)}, bf16[256,512]{1,0:T(8,128)(2,1)S(1)}, u32[]{:S(2)}, u32[]{:S(2)}) collective-permute-start(bf16[256,512]{1,0:T(8,128)(2,1)} %og_ref.1), channel_id=1, source_target_pairs={{0,1},{1,0},{2,3},{3,2},{4,5},{5,4},{6,7},{7,6},{8,9},{9,8},{10,11... | collective-permute-start | bytes 786440 | tf_op jit(solution)/shard_map/ppermute | solution.py:347
  3.2 1.0 copy-done
  4.2 1.0 copy-done.4
  5.2 0.9 copy-done.7
  6.2 1.9 %shard_map.129 = bf16[8,288,512]{2,1,0:T(8,128)(2,1)} custom-call(bf16[256,512]{1,0:T(8,128)(2,1)S(1)} %copy-done.7, bf16[256,512]{1,0:T(8,128)(2,1)S(1)} %copy-done, bf16[512,512]{1,0:T(8,128)(2,1)S(1)} %copy-done.4), custom_call_target="tpu_custom_call" | custom-call | tf_op jit(solution)/shard_map/pallas_call | solution.py:403
  8.1 4.5 %all-to-all-start = ((bf16[8,288,512]{2,1,0:T(8,128)(2,1)}), bf16[8,288,512]{2,1,0:T(8,128)(2,1)}, u32[]{:S(2)}, u32[]{:S(2)}) async-start(bf16[8,288,512]{2,1,0:T(8,128)(2,1)} %shard_map.129), calls=%async_computation | async-start | bytes 4718592 | tf_op jit(solution)/shard_map/all_to_all | solution.py:417
  12.7 0.1 convert_reduce_fusion
  12.9 0.2 select_reduce_fusion
  13.2 0.1 select_reduce_fusion.1
  13.8 1.0 collective-permute-start.1
  15.1 2.5 %copy.64 = bf16[512,2048]{0,1:T(8,128)(2,1)} copy(bf16[512,2048]{1,0:T(8,128)(2,1)S(1)} %copy-done.9) | data formatting | bytes 4194304 | tf_op args[2]
  17.7 0.6 fusion.14
  20.2 0.7 select_select_fusion
  20.8 1.0 dynamic-slice_bitcast_fusion.1
  21.9 0.2 broadcast_select_fusion.lo_ref
  22.3 1.4 collective-permute-start.4
  23.6 2.6 %collective-permute-start.3 = (s32[2,4,32]{2,1,0:T(4,128)S(1)}, s32[2,4,32]{2,1,0:T(4,128)S(1)}, u32[]{:S(2)}, u32[]{:S(2)}) collective-permute-start(s32[2,4,32]{2,1,0:T(4,128)S(1)} %get-tuple-element.102), channel_id=1, source_target_pairs={{0,128},{8,136},{16,144},{24,152},{32,160},{40,168},{48,176},{56,1... | collective-permute-start | bytes 3080 | tf_op jit(solution)/shard_map/ppermute | solution.py:317
  26.3 1.1 collective-permute-start.2
  27.3 1.8 %collective-permute-done.2 = s32[2,4,32]{2,1,0:T(4,128)S(1)} collective-permute-done((s32[2,4,32]{2,1,0:T(4,128)S(1)}, s32[2,4,32]{2,1,0:T(4,128)S(1)}, u32[]{:S(2)}, u32[]{:S(2)}) %collective-permute-start.2) | collective-permute-done | bytes 1056 | tf_op jit(solution)/shard_map/ppermute | solution.py:317
  29.3 6.5 %collective-permute-start.6 = (s32[4,2,32]{2,1,0:T(2,128)S(1)}, s32[4,2,32]{2,1,0:T(2,128)S(1)}, u32[]{:S(2)}, u32[]{:S(2)}) collective-permute-start(s32[4,2,32]{2,1,0:T(2,128)S(1)} %bitcast.162), channel_id=1, source_target_pairs={{0,32},{8,40},{16,48},{24,56},{32,0},{40,8},{48,16},{56,24},{64,96... | collective-permute-start | bytes 3080 | tf_op jit(solution)/shard_map/ppermute | solution.py:317
  35.7 2.4 %collective-permute-start.5 = (s32[4,2,32]{2,1,0:T(2,128)S(1)}, s32[4,2,32]{2,1,0:T(2,128)S(1)}, u32[]{:S(2)}, u32[]{:S(2)}) collective-permute-start(s32[4,2,32]{2,1,0:T(2,128)S(1)} %bitcast.160), channel_id=1, source_target_pairs={{0,16},{8,24},{16,32},{24,40},{32,48},{40,56},{48,0},{56,8},{64,80... | collective-permute-start | bytes 3080 | tf_op jit(solution)/shard_map/ppermute | solution.py:317
  38.1 3.5 %all-to-all-done.r_ref = bf16[8,288,512]{2,1,0:T(8,128)(2,1)} async-done(((bf16[8,288,512]{2,1,0:T(8,128)(2,1)}), bf16[8,288,512]{2,1,0:T(8,128)(2,1)}, u32[]{:S(2)}, u32[]{:S(2)}) %all-to-all-start) | async-done | bytes 2359328 | tf_op jit(solution)/shard_map/all_to_all | solution.py:417
  41.6 1.3 collective-permute-start.9
  42.9 9.8 %shard_map.130 = (bf16[256,2048]{1,0:T(8,128)(2,1)S(1)}, f32[256,2048]{1,0:T(8,128)}, f32[64,2048]{1,0:T(8,128)S(1)}, f32[8,4,2048]{2,1,0:T(4,128)}) custom-call(s32[4]{0:T(128)S(1)} %bitcast.139, bf16[8,288,512]{2,1,0:T(8,128)(2,1)} %all-to-all-done.r_ref, bf16[256,512]{1,0:T(8,128)(2,1)S(1)} %bitcast.138, s32[16,1,2048]{2,1,0:T(1,128)S(1)} %broadcast_select_fusion.lo_ref), custom_call_target="tpu_custom_call" | custom-call | tf_op jit(solution)/shard_map/pallas_call | solution.py:444
  52.7 1.0 copy-done.2
  53.7 4.2 %all-to-all-start.1 = ((f32[8,4,2048]{2,1,0:T(4,128)}), f32[8,4,2048]{2,1,0:T(4,128)S(1)}, u32[]{:S(2)}, u32[]{:S(2)}) async-start(f32[8,4,2048]{2,1,0:T(4,128)} %get-tuple-element.52), calls=%async_computation.1 | async-start | bytes 524288 | tf_op jit(solution)/shard_map/all_to_all | solution.py:452
  58.1 0.3 copy.67
  58.4 5.6 %all-to-all-done.1.st_ref = f32[8,4,2048]{2,1,0:T(4,128)S(1)} async-done(((f32[8,4,2048]{2,1,0:T(4,128)}), f32[8,4,2048]{2,1,0:T(4,128)S(1)}, u32[]{:S(2)}, u32[]{:S(2)}) %all-to-all-start.1) | async-done | bytes 262176 | tf_op jit(solution)/shard_map/all_to_all | solution.py:452
  64.1 0.3 collective-permute-start.11
  64.4 1.1 collective-permute-start.10
  65.5 1.2 copy-done.3
  66.7 12.8 %shard_map.131 = (bf16[8,272,256]{2,1,0:T(8,128)(2,1)}, bf16[64,2048]{1,0:T(8,128)(2,1)S(1)}) custom-call(s32[4]{0:T(128)S(1)} %bitcast.140, f32[8,4,2048]{2,1,0:T(4,128)S(1)} %all-to-all-done.1.st_ref, bf16[8,288,512]{2,1,0:T(8,128)(2,1)} %all-to-all-done.r_ref, s32[16,1,2048]{2,1,0:T(1,128)S(1)} %broadcast_select_fusion.lo_ref, ...), custom_call_target="tpu_custom_call" | custom-call | tf_op jit(solution)/shard_map/pallas_call | solution.py:456
  79.5 0.7 copy-done.5
  80.2 3.7 %all-to-all-start.2 = ((bf16[8,272,256]{2,1,0:T(8,128)(2,1)}), bf16[8,272,256]{2,1,0:T(8,128)(2,1)S(1)}, u32[]{:S(2)}, u32[]{:S(2)}) async-start(bf16[8,272,256]{2,1,0:T(8,128)(2,1)} %get-tuple-element.65.gp_ref), calls=%async_computation.2 | async-start | bytes 2228224 | tf_op jit(solution)/shard_map/all_to_all | solution.py:471
  84.0 0.9 copy-done.6
  84.9 3.2 %shard_map.132 = f32[1280,128]{1,0:T(8,128)S(1)} custom-call(s32[1]{0:T(128)} %bitcast.45.place_ref, bf16[8,272,256]{2,1,0:T(8,128)(2,1)} %get-tuple-element.65.gp_ref, bf16[8,288,512]{2,1,0:T(8,128)(2,1)} %all-to-all-done.r_ref, bf16[64,2048]{1,0:T(8,128)(2,1)S(1)} %copy-done.6, bf16[2,256,512]{2,1,0:T(8,128)(2,1)S(1)} %pad_maximum_fusion.refs_0_, ...), custom_call_target="tpu_custom_call" | custom-call | tf_op jit(solution)/shard_map/pallas_call | solution.py:475
  88.2 8.3 %collective-permute-start.12 = (f32[640,128]{1,0:T(8,128)S(1)}, f32[640,128]{1,0:T(8,128)S(1)}, u32[]{:S(2)}, u32[]{:S(2)}) collective-permute-start(f32[640,128]{1,0:T(8,128)S(1)} %dynamic-slice_bitcast_fusion), channel_id=1, source_target_pairs={{0,8},{8,0},{16,24},{24,16},{32,40},{40,32},{48,56},{56,48},{64,72... | collective-permute-start | bytes 983048 | tf_op jit(solution)/shard_map/ppermute | solution.py:359
  96.5 1.3 collective-permute-done.12
  97.8 1.6 collective-permute-start.13
  99.4 1.1 collective-permute-start.15
  100.6 0.7 collective-permute-start.14
  101.3 1.4 collective-permute-done.13
  102.8 0.3 collective-permute-done.15
  103.0 2.3 %collective-permute-done.14 = f32[160,128]{1,0:T(8,128)S(1)} collective-permute-done((f32[160,128]{1,0:T(8,128)S(1)}, f32[160,128]{1,0:T(8,128)S(1)}, u32[]{:S(2)}, u32[]{:S(2)}) %collective-permute-start.14) | collective-permute-done | bytes 81952 | tf_op jit(solution)/shard_map/ppermute | solution.py:304
  105.4 3.9 %collective-permute-start.18 = (f32[160,128]{1,0:T(8,128)S(1)}, f32[160,128]{1,0:T(8,128)S(1)}, u32[]{:S(2)}, u32[]{:S(2)}) collective-permute-start(f32[160,128]{1,0:T(8,128)S(1)} %fusion.3), channel_id=1, source_target_pairs={{0,48},{8,56},{16,0},{24,8},{32,16},{40,24},{48,32},{56,40},{64,11... | collective-permute-start | bytes 245768 | tf_op jit(solution)/shard_map/ppermute | solution.py:309
  109.3 2.1 %collective-permute-start.16 = (f32[160,128]{1,0:T(8,128)S(1)}, f32[160,128]{1,0:T(8,128)S(1)}, u32[]{:S(2)}, u32[]{:S(2)}) collective-permute-start(f32[160,128]{1,0:T(8,128)S(1)} %fusion.3), channel_id=1, source_target_pairs={{0,16},{8,24},{16,32},{24,40},{32,48},{40,56},{48,0},{56,8},{64,80... | collective-permute-start | bytes 245768 | tf_op jit(solution)/shard_map/ppermute | solution.py:309
  111.4 4.6 %shard_map.133 = bf16[256,16,128]{2,1,0:T(8,128)(2,1)} custom-call(bf16[8,272,256]{2,1,0:T(8,128)(2,1)S(1)} %all-to-all-done.2.back_ref, bf16[512,2048]{1,0:T(8,128)(2,1)} %w_ref.1, bf16[256,512]{1,0:T(8,128)(2,1)S(1)} %copy-done.1, s32[1,256]{1,0:T(1,128)S(1)} %bitcast.142, s32[1,256]{1,0:T(1,128)S(1)} %bitcast.141), custom_call_target="tpu_custom_call" | custom-call | tf_op jit(solution)/shard_map/pallas_call | solution.py:481
  115.9 1.8 %collective-permute-done.17 = f32[160,128]{1,0:T(8,128)S(1)} collective-permute-done((f32[160,128]{1,0:T(8,128)S(1)}, f32[160,128]{1,0:T(8,128)S(1)}, u32[]{:S(2)}, u32[]{:S(2)}) %collective-permute-start.17) | collective-permute-done | bytes 81952 | tf_op jit(solution)/shard_map/ppermute | solution.py:309
  117.8 0.2 collective-permute-start.19
  118.0 2.7 %collective-permute-done.19 = bf16[160,128]{1,0:T(8,128)(2,1)S(1)} collective-permute-done((bf16[160,128]{1,0:T(8,128)(2,1)S(1)}, bf16[160,128]{1,0:T(8,128)(2,1)S(1)}, u32[]{:S(2)}, u32[]{:S(2)}) %collective-permute-start.19) | collective-permute-done | bytes 40992 | tf_op jit(solution)/shard_map/ppermute | solution.py:347
  120.7 13.7 %all-to-all-start.3 = ((bf16[256,16,128]{2,1,0:T(8,128)(2,1)}), bf16[256,16,128]{2,1,0:T(8,128)(2,1)S(1)}, u32[]{:S(2)}, u32[]{:S(2)}) async-start(bf16[256,16,128]{2,1,0:T(8,128)(2,1)} %shard_map.133), calls=%async_computation.3 | async-start | bytes 2097152 | tf_op jit(solution)/shard_map/all_to_all | solution.py:491
  134.4 2.7 %collective-permute-start.22 = (bf16[2,160,128]{2,1,0:T(8,128)(2,1)S(1)}, bf16[2,160,128]{2,1,0:T(8,128)(2,1)S(1)}, u32[]{:S(2)}, u32[]{:S(2)}) collective-permute-start(bf16[2,160,128]{2,1,0:T(8,128)(2,1)S(1)} %pad_maximum_fusion.2), channel_id=1, source_target_pairs={{0,6},{1,7},{2,4},{3,5},{4,2},{5,3},{6,0},{7,1},{8,14},{9,15},{10,... | collective-permute-start | bytes 245768 | tf_op jit(solution)/shard_map/ppermute | solution.py:347
  137.1 0.6 collective-permute-start.21
  137.8 5.4 %collective-permute-done.20 = bf16[2,160,128]{2,1,0:T(8,128)(2,1)S(1)} collective-permute-done((bf16[2,160,128]{2,1,0:T(8,128)(2,1)S(1)}, bf16[2,160,128]{2,1,0:T(8,128)(2,1)S(1)}, u32[]{:S(2)}, u32[]{:S(2)}) %collective-permute-start.20) | collective-permute-done | bytes 81952 | tf_op jit(solution)/shard_map/ppermute | solution.py:347
  143.2 0.3 collective-permute-done.21
  143.6 3.0 %collective-permute-start.25 = (bf16[8,160,128]{2,1,0:T(8,128)(2,1)S(1)}, bf16[8,160,128]{2,1,0:T(8,128)(2,1)S(1)}, u32[]{:S(2)}, u32[]{:S(2)}) collective-permute-start(bf16[8,160,128]{2,1,0:T(8,128)(2,1)S(1)} %constant_dynamic-update-slice_fusion.16.refs_0_), channel_id=1, source_target_pairs={{0,192},{8,200},{16,208},{24,216},{32,224},{40,232},{48,240},{56,2... | collective-permute-start | bytes 983048 | tf_op jit(solution)/shard_map/ppermute | solution.py:343
  146.8 10.6 %collective-permute-done.25.refs_4_ = bf16[8,160,128]{2,1,0:T(8,128)(2,1)S(1)} collective-permute-done((bf16[8,160,128]{2,1,0:T(8,128)(2,1)S(1)}, bf16[8,160,128]{2,1,0:T(8,128)(2,1)S(1)}, u32[]{:S(2)}, u32[]{:S(2)}) %collective-permute-start.25) | collective-permute-done | bytes 327712 | tf_op jit(solution)/shard_map/ppermute | solution.py:343
  157.5 1.0 collective-permute-start.26
  158.5 1.9 %collective-permute-start.24 = (bf16[4,160,128]{2,1,0:T(8,128)(2,1)S(1)}, bf16[4,160,128]{2,1,0:T(8,128)(2,1)S(1)}, u32[]{:S(2)}, u32[]{:S(2)}) collective-permute-start(bf16[4,160,128]{2,1,0:T(8,128)(2,1)S(1)} %slice.78), channel_id=1, source_target_pairs={{0,192},{8,200},{16,208},{24,216},{32,224},{40,232},{48,240},{56,2... | collective-permute-start | bytes 491528 | tf_op jit(solution)/shard_map/ppermute | solution.py:343
  160.9 5.7 %all-to-all-done.3.in_ref = bf16[256,16,128]{2,1,0:T(8,128)(2,1)S(1)} async-done(((bf16[256,16,128]{2,1,0:T(8,128)(2,1)}), bf16[256,16,128]{2,1,0:T(8,128)(2,1)S(1)}, u32[]{:S(2)}, u32[]{:S(2)}) %all-to-all-start.3) | async-done | bytes 1048608 | tf_op jit(solution)/shard_map/all_to_all | solution.py:491
  166.7 2.2 %shard_map.134 = (f32[512,512]{1,0:T(8,128)}, f32[512,512]{1,0:T(8,128)}) custom-call(bf16[256,16,128]{2,1,0:T(8,128)(2,1)S(1)} %all-to-all-done.3.in_ref, s32[512,1]{1,0:T(8,128)S(1)} %reshape_squeeze.8.qc_ref, s32[1,512]{1,0:T(1,128)S(1)} %bitcast.144, s32[512,1]{1,0:T(8,128)S(1)} %reshape_squeeze.9.rc_ref, s32[1,512]{1,0:T(1,128)S(1)} %bitcast.143), custom_call_target="tpu_custom_call" | custom-call | tf_op jit(solution)/shard_map/pallas_call | solution.py:497
  169.0 0.5 collective-permute-start.27
  169.5 2.7 %collective-permute-done.27.other_ref = bf16[8,640,128]{2,1,0:T(8,128)(2,1)S(1)} collective-permute-done((bf16[8,640,128]{2,1,0:T(8,128)(2,1)S(1)}, bf16[8,640,128]{2,1,0:T(8,128)(2,1)S(1)}, u32[]{:S(2)}, u32[]{:S(2)}) %collective-permute-start.27) | collective-permute-done | bytes 1310752 | tf_op jit(solution)/shard_map/ppermute | solution.py:364
  172.2 3.2 %shard_map.136 = (f32[512,2048]{1,0:T(8,128)}, f32[512,512]{1,0:T(8,128)}) custom-call(s32[1]{0:T(128)} %bitcast.64.core_ref, bf16[8,640,128]{2,1,0:T(8,128)(2,1)S(1)} %shard_map.135.mine_ref, bf16[8,640,128]{2,1,0:T(8,128)(2,1)S(1)} %collective-permute-done.27.other_ref), custom_call_target="tpu_custom_call" | custom-call | tf_op jit(solution)/shard_map/pallas_call | solution.py:366
  (117 shorter events, 2.6 us)
Async XLA Ops:
  0.6 37.4 %collective-permute-start = (bf16[256,512]{1,0:T(8,128)(2,1)}, bf16[256,512]{1,0:T(8,128)(2,1)S(1)}, u32[]{:S(2)}, u32[]{:S(2)}) collective-permute-start(bf16[256,512]{1,0:T(8,128)(2,1)} %og_ref.1), channel_id=1, source_target_pairs={{0,1},{1,0},{2,3},{3,2},{4,5},{5,4},{6,7},{7,6},{8,9},{9,8},{10,11... | collective-permute-start | bytes 786440 | tf_op jit(solution)/shard_map/ppermute | solution.py:347
  3.2 1.0 copy-start
  4.2 1.0 copy-start.4
  5.2 0.9 copy-start.7
  8.1 4.6 %copy-start.13 = (s32[256]{0:T(256)S(1)}, s32[256]{0:T(256)}, u32[]{:S(2)}) copy-start(s32[256]{0:T(256)} %param.19) | copy-start | bytes 3076
  8.1 4.6 %copy-start.10 = (s32[256]{0:T(256)S(1)}, s32[256]{0:T(256)}, u32[]{:S(2)}) copy-start(s32[256]{0:T(256)} %param.18) | copy-start | bytes 3076
  8.1 4.6 %copy-start.11 = (s32[256]{0:T(256)S(1)}, s32[256]{0:T(256)}, u32[]{:S(2)}) copy-start(s32[256]{0:T(256)} %param.16) | copy-start | bytes 3076
  8.1 4.9 %copy-start.14 = (s32[256]{0:T(256)S(1)}, s32[256]{0:T(256)}, u32[]{:S(2)}) copy-start(s32[256]{0:T(256)} %param.17) | copy-start | bytes 3076
  8.1 6.7 %copy-start.12 = (s32[16,16]{1,0:T(8,128)S(1)}, s32[16,16]{1,0:T(8,128)}, u32[]{:S(2)}) copy-start(s32[16,16]{1,0:T(8,128)} %param.15) | copy-start | bytes 3076
  8.1 7.0 %copy-start.9 = (bf16[512,2048]{1,0:T(8,128)(2,1)S(1)}, bf16[512,2048]{1,0:T(8,128)(2,1)}, u32[]{:S(2)}) copy-start(bf16[512,2048]{1,0:T(8,128)(2,1)} %w_ref.1) | copy-start | bytes 6291460
  8.1 33.4 %all-to-all-start = ((bf16[8,288,512]{2,1,0:T(8,128)(2,1)}), bf16[8,288,512]{2,1,0:T(8,128)(2,1)}, u32[]{:S(2)}, u32[]{:S(2)}) async-start(bf16[8,288,512]{2,1,0:T(8,128)(2,1)} %shard_map.129), calls=%async_computation | async-start | bytes 4718592 | tf_op jit(solution)/shard_map/all_to_all | solution.py:417
  13.8 8.4 %collective-permute-start.1 = (s32[4,4,32]{2,1,0:T(4,128)S(1)}, s32[4,4,32]{2,1,0:T(4,128)S(1)}, u32[]{:S(2)}, u32[]{:S(2)}) collective-permute-start(s32[4,4,32]{2,1,0:T(4,128)S(1)} %bitcast.158), channel_id=1, source_target_pairs={{0,8},{8,0},{16,24},{24,16},{32,40},{40,32},{48,56},{56,48},{64,72... | collective-permute-start | bytes 6152 | tf_op jit(solution)/shard_map/ppermute | solution.py:317
  15.1 2.5 %copy-start.8 = (s32[1,4]{1,0:T(1,128)S(1)}, s32[1,4]{1,0:T(1,128)}, u32[]{:S(2)}) copy-start(s32[1,4]{1,0:T(1,128)} %param.14) | copy-start | bytes 52
  17.7 23.9 %copy-start.1 = (bf16[256,512]{1,0:T(8,128)(2,1)S(1)}, bf16[256,512]{1,0:T(8,128)(2,1)}, u32[]{:S(2)}) copy-start(bf16[256,512]{1,0:T(8,128)(2,1)} %og_ref.1) | copy-start | bytes 786436
  22.3 6.9 %collective-permute-start.4 = (s32[2,4,32]{2,1,0:T(4,128)S(1)}, s32[2,4,32]{2,1,0:T(4,128)S(1)}, u32[]{:S(2)}, u32[]{:S(2)}) collective-permute-start(s32[2,4,32]{2,1,0:T(4,128)S(1)} %get-tuple-element.101), channel_id=1, source_target_pairs={{0,64},{8,72},{16,80},{24,88},{32,96},{40,104},{48,112},{56,120},{... | collective-permute-start | bytes 3080 | tf_op jit(solution)/shard_map/ppermute | solution.py:317
  23.6 5.5 %collective-permute-start.3 = (s32[2,4,32]{2,1,0:T(4,128)S(1)}, s32[2,4,32]{2,1,0:T(4,128)S(1)}, u32[]{:S(2)}, u32[]{:S(2)}) collective-permute-start(s32[2,4,32]{2,1,0:T(4,128)S(1)} %get-tuple-element.102), channel_id=1, source_target_pairs={{0,128},{8,136},{16,144},{24,152},{32,160},{40,168},{48,176},{56,1... | collective-permute-start | bytes 3080 | tf_op jit(solution)/shard_map/ppermute | solution.py:317
  26.3 2.9 %collective-permute-start.2 = (s32[2,4,32]{2,1,0:T(4,128)S(1)}, s32[2,4,32]{2,1,0:T(4,128)S(1)}, u32[]{:S(2)}, u32[]{:S(2)}) collective-permute-start(s32[2,4,32]{2,1,0:T(4,128)S(1)} %get-tuple-element.103), channel_id=1, source_target_pairs={{0,192},{8,200},{16,208},{24,216},{32,224},{40,232},{48,240},{56,2... | collective-permute-start | bytes 3080 | tf_op jit(solution)/shard_map/ppermute | solution.py:317
  29.3 24.4 %collective-permute-start.6 = (s32[4,2,32]{2,1,0:T(2,128)S(1)}, s32[4,2,32]{2,1,0:T(2,128)S(1)}, u32[]{:S(2)}, u32[]{:S(2)}) collective-permute-start(s32[4,2,32]{2,1,0:T(2,128)S(1)} %bitcast.162), channel_id=1, source_target_pairs={{0,32},{8,40},{16,48},{24,56},{32,0},{40,8},{48,16},{56,24},{64,96... | collective-permute-start | bytes 3080 | tf_op jit(solution)/shard_map/ppermute | solution.py:317
  35.7 18.0 %collective-permute-start.7 = (s32[4,2,32]{2,1,0:T(2,128)S(1)}, s32[4,2,32]{2,1,0:T(2,128)S(1)}, u32[]{:S(2)}, u32[]{:S(2)}) collective-permute-start(s32[4,2,32]{2,1,0:T(2,128)S(1)} %bitcast.161), channel_id=1, source_target_pairs={{0,48},{8,56},{16,0},{24,8},{32,16},{40,24},{48,32},{56,40},{64,11... | collective-permute-start | bytes 3080 | tf_op jit(solution)/shard_map/ppermute | solution.py:317
  35.7 18.0 %collective-permute-start.5 = (s32[4,2,32]{2,1,0:T(2,128)S(1)}, s32[4,2,32]{2,1,0:T(2,128)S(1)}, u32[]{:S(2)}, u32[]{:S(2)}) collective-permute-start(s32[4,2,32]{2,1,0:T(2,128)S(1)} %bitcast.160), channel_id=1, source_target_pairs={{0,16},{8,24},{16,32},{24,40},{32,48},{40,56},{48,0},{56,8},{64,80... | collective-permute-start | bytes 3080 | tf_op jit(solution)/shard_map/ppermute | solution.py:317
  41.6 22.4 %collective-permute-start.9 = (bf16[2,256,512]{2,1,0:T(8,128)(2,1)S(1)}, bf16[2,256,512]{2,1,0:T(8,128)(2,1)S(1)}, u32[]{:S(2)}, u32[]{:S(2)}) collective-permute-start(bf16[2,256,512]{2,1,0:T(8,128)(2,1)S(1)} %pad_maximum_fusion.refs_0_), channel_id=1, source_target_pairs={{0,6},{1,7},{2,4},{3,5},{4,2},{5,3},{6,0},{7,1},{8,14},{9,15},{10,... | collective-permute-start | bytes 1572872 | tf_op jit(solution)/shard_map/ppermute | solution.py:347
  42.9 21.2 %collective-permute-start.8 = (bf16[2,256,512]{2,1,0:T(8,128)(2,1)S(1)}, bf16[2,256,512]{2,1,0:T(8,128)(2,1)S(1)}, u32[]{:S(2)}, u32[]{:S(2)}) collective-permute-start(bf16[2,256,512]{2,1,0:T(8,128)(2,1)S(1)} %pad_maximum_fusion.refs_0_), channel_id=1, source_target_pairs={{0,2},{1,3},{2,0},{3,1},{4,6},{5,7},{6,4},{7,5},{8,10},{9,11},{10,... | collective-permute-start | bytes 1572872 | tf_op jit(solution)/shard_map/ppermute | solution.py:347
  52.7 1.0 copy-start.2
  53.7 10.3 %all-to-all-start.1 = ((f32[8,4,2048]{2,1,0:T(4,128)}), f32[8,4,2048]{2,1,0:T(4,128)S(1)}, u32[]{:S(2)}, u32[]{:S(2)}) async-start(f32[8,4,2048]{2,1,0:T(4,128)} %get-tuple-element.52), calls=%async_computation.1 | async-start | bytes 524288 | tf_op jit(solution)/shard_map/all_to_all | solution.py:452
  64.1 16.2 %collective-permute-start.11 = (bf16[256,512]{1,0:T(8,128)(2,1)S(1)}, bf16[256,512]{1,0:T(8,128)(2,1)S(1)}, u32[]{:S(2)}, u32[]{:S(2)}) collective-permute-start(bf16[256,512]{1,0:T(8,128)(2,1)S(1)} %slice_bitcast_fusion), channel_id=1, source_target_pairs={{0,2},{1,3},{2,0},{3,1},{4,6},{5,7},{6,4},{7,5},{8,10},{9,11},{10,... | collective-permute-start | bytes 786440 | tf_op jit(solution)/shard_map/ppermute | solution.py:347
  64.4 15.9 %collective-permute-start.10 = (bf16[256,512]{1,0:T(8,128)(2,1)S(1)}, bf16[256,512]{1,0:T(8,128)(2,1)S(1)}, u32[]{:S(2)}, u32[]{:S(2)}) collective-permute-start(bf16[256,512]{1,0:T(8,128)(2,1)S(1)} %slice_bitcast_fusion.1), channel_id=1, source_target_pairs={{0,6},{1,7},{2,4},{3,5},{4,2},{5,3},{6,0},{7,1},{8,14},{9,15},{10,... | collective-permute-start | bytes 786440 | tf_op jit(solution)/shard_map/ppermute | solution.py:347
  65.5 1.2 copy-start.3
  79.5 0.7 copy-start.5
  80.2 25.2 %all-to-all-start.2 = ((bf16[8,272,256]{2,1,0:T(8,128)(2,1)}), bf16[8,272,256]{2,1,0:T(8,128)(2,1)S(1)}, u32[]{:S(2)}, u32[]{:S(2)}) async-start(bf16[8,272,256]{2,1,0:T(8,128)(2,1)} %get-tuple-element.65.gp_ref), calls=%async_computation.2 | async-start | bytes 2228224 | tf_op jit(solution)/shard_map/all_to_all | solution.py:471
  84.0 0.9 copy-start.6
  88.2 9.6 %collective-permute-start.12 = (f32[640,128]{1,0:T(8,128)S(1)}, f32[640,128]{1,0:T(8,128)S(1)}, u32[]{:S(2)}, u32[]{:S(2)}) collective-permute-start(f32[640,128]{1,0:T(8,128)S(1)} %dynamic-slice_bitcast_fusion), channel_id=1, source_target_pairs={{0,8},{8,0},{16,24},{24,16},{32,40},{40,32},{48,56},{56,48},{64,72... | collective-permute-start | bytes 983048 | tf_op jit(solution)/shard_map/ppermute | solution.py:359
  97.8 4.9 %collective-permute-start.13 = (f32[160,128]{1,0:T(8,128)S(1)}, f32[160,128]{1,0:T(8,128)S(1)}, u32[]{:S(2)}, u32[]{:S(2)}) collective-permute-start(f32[160,128]{1,0:T(8,128)S(1)} %get-tuple-element.90), channel_id=1, source_target_pairs={{0,64},{8,72},{16,80},{24,88},{32,96},{40,104},{48,112},{56,120},{... | collective-permute-start | bytes 245768 | tf_op jit(solution)/shard_map/ppermute | solution.py:304
  99.4 3.6 %collective-permute-start.15 = (f32[160,128]{1,0:T(8,128)S(1)}, f32[160,128]{1,0:T(8,128)S(1)}, u32[]{:S(2)}, u32[]{:S(2)}) collective-permute-start(f32[160,128]{1,0:T(8,128)S(1)} %get-tuple-element.91), channel_id=1, source_target_pairs={{0,192},{8,200},{16,208},{24,216},{32,224},{40,232},{48,240},{56,2... | collective-permute-start | bytes 245768 | tf_op jit(solution)/shard_map/ppermute | solution.py:304
  100.6 4.8 %collective-permute-start.14 = (f32[160,128]{1,0:T(8,128)S(1)}, f32[160,128]{1,0:T(8,128)S(1)}, u32[]{:S(2)}, u32[]{:S(2)}) collective-permute-start(f32[160,128]{1,0:T(8,128)S(1)} %get-tuple-element.92), channel_id=1, source_target_pairs={{0,128},{8,136},{16,144},{24,152},{32,160},{40,168},{48,176},{56,1... | collective-permute-start | bytes 245768 | tf_op jit(solution)/shard_map/ppermute | solution.py:304
  105.4 10.5 %collective-permute-start.18 = (f32[160,128]{1,0:T(8,128)S(1)}, f32[160,128]{1,0:T(8,128)S(1)}, u32[]{:S(2)}, u32[]{:S(2)}) collective-permute-start(f32[160,128]{1,0:T(8,128)S(1)} %fusion.3), channel_id=1, source_target_pairs={{0,48},{8,56},{16,0},{24,8},{32,16},{40,24},{48,32},{56,40},{64,11... | collective-permute-start | bytes 245768 | tf_op jit(solution)/shard_map/ppermute | solution.py:309
  109.3 8.5 %collective-permute-start.17 = (f32[160,128]{1,0:T(8,128)S(1)}, f32[160,128]{1,0:T(8,128)S(1)}, u32[]{:S(2)}, u32[]{:S(2)}) collective-permute-start(f32[160,128]{1,0:T(8,128)S(1)} %fusion.3), channel_id=1, source_target_pairs={{0,32},{8,40},{16,48},{24,56},{32,0},{40,8},{48,16},{56,24},{64,96... | collective-permute-start | bytes 245768 | tf_op jit(solution)/shard_map/ppermute | solution.py:309
  109.3 8.5 %collective-permute-start.16 = (f32[160,128]{1,0:T(8,128)S(1)}, f32[160,128]{1,0:T(8,128)S(1)}, u32[]{:S(2)}, u32[]{:S(2)}) collective-permute-start(f32[160,128]{1,0:T(8,128)S(1)} %fusion.3), channel_id=1, source_target_pairs={{0,16},{8,24},{16,32},{24,40},{32,48},{40,56},{48,0},{56,8},{64,80... | collective-permute-start | bytes 245768 | tf_op jit(solution)/shard_map/ppermute | solution.py:309
  117.8 2.9 %collective-permute-start.19 = (bf16[160,128]{1,0:T(8,128)(2,1)S(1)}, bf16[160,128]{1,0:T(8,128)(2,1)S(1)}, u32[]{:S(2)}, u32[]{:S(2)}) collective-permute-start(bf16[160,128]{1,0:T(8,128)(2,1)S(1)} %add_convert_fusion), channel_id=1, source_target_pairs={{0,1},{1,0},{2,3},{3,2},{4,5},{5,4},{6,7},{7,6},{8,9},{9,8},{10,11... | collective-permute-start | bytes 122888 | tf_op jit(solution)/shard_map/ppermute | solution.py:347
  120.7 45.9 %all-to-all-start.3 = ((bf16[256,16,128]{2,1,0:T(8,128)(2,1)}), bf16[256,16,128]{2,1,0:T(8,128)(2,1)S(1)}, u32[]{:S(2)}, u32[]{:S(2)}) async-start(bf16[256,16,128]{2,1,0:T(8,128)(2,1)} %shard_map.133), calls=%async_computation.3 | async-start | bytes 2097152 | tf_op jit(solution)/shard_map/all_to_all | solution.py:491
  134.4 9.1 %collective-permute-start.22 = (bf16[2,160,128]{2,1,0:T(8,128)(2,1)S(1)}, bf16[2,160,128]{2,1,0:T(8,128)(2,1)S(1)}, u32[]{:S(2)}, u32[]{:S(2)}) collective-permute-start(bf16[2,160,128]{2,1,0:T(8,128)(2,1)S(1)} %pad_maximum_fusion.2), channel_id=1, source_target_pairs={{0,6},{1,7},{2,4},{3,5},{4,2},{5,3},{6,0},{7,1},{8,14},{9,15},{10,... | collective-permute-start | bytes 245768 | tf_op jit(solution)/shard_map/ppermute | solution.py:347
  137.1 6.4 %collective-permute-start.21 = (bf16[2,160,128]{2,1,0:T(8,128)(2,1)S(1)}, bf16[2,160,128]{2,1,0:T(8,128)(2,1)S(1)}, u32[]{:S(2)}, u32[]{:S(2)}) collective-permute-start(bf16[2,160,128]{2,1,0:T(8,128)(2,1)S(1)} %pad_maximum_fusion.2), channel_id=1, source_target_pairs={{0,4},{1,5},{2,6},{3,7},{4,0},{5,1},{6,2},{7,3},{8,12},{9,13},{10,... | collective-permute-start | bytes 245768 | tf_op jit(solution)/shard_map/ppermute | solution.py:347
  137.7 5.5 %collective-permute-start.20 = (bf16[2,160,128]{2,1,0:T(8,128)(2,1)S(1)}, bf16[2,160,128]{2,1,0:T(8,128)(2,1)S(1)}, u32[]{:S(2)}, u32[]{:S(2)}) collective-permute-start(bf16[2,160,128]{2,1,0:T(8,128)(2,1)S(1)} %pad_maximum_fusion.2), channel_id=1, source_target_pairs={{0,2},{1,3},{2,0},{3,1},{4,6},{5,7},{6,4},{7,5},{8,10},{9,11},{10,... | collective-permute-start | bytes 245768 | tf_op jit(solution)/shard_map/ppermute | solution.py:347
  143.6 13.9 %collective-permute-start.25 = (bf16[8,160,128]{2,1,0:T(8,128)(2,1)S(1)}, bf16[8,160,128]{2,1,0:T(8,128)(2,1)S(1)}, u32[]{:S(2)}, u32[]{:S(2)}) collective-permute-start(bf16[8,160,128]{2,1,0:T(8,128)(2,1)S(1)} %constant_dynamic-update-slice_fusion.16.refs_0_), channel_id=1, source_target_pairs={{0,192},{8,200},{16,208},{24,216},{32,224},{40,232},{48,240},{56,2... | collective-permute-start | bytes 983048 | tf_op jit(solution)/shard_map/ppermute | solution.py:343
  146.6 11.9 %collective-permute-start.23 = (bf16[8,160,128]{2,1,0:T(8,128)(2,1)S(1)}, bf16[8,160,128]{2,1,0:T(8,128)(2,1)S(1)}, u32[]{:S(2)}, u32[]{:S(2)}) collective-permute-start(bf16[8,160,128]{2,1,0:T(8,128)(2,1)S(1)} %constant_dynamic-update-slice_fusion.16.refs_0_), channel_id=1, source_target_pairs={{0,64},{8,72},{16,80},{24,88},{32,96},{40,104},{48,112},{56,120},{... | collective-permute-start | bytes 983048 | tf_op jit(solution)/shard_map/ppermute | solution.py:343
  157.5 11.4 %collective-permute-start.26 = (bf16[4,160,128]{2,1,0:T(8,128)(2,1)S(1)}, bf16[4,160,128]{2,1,0:T(8,128)(2,1)S(1)}, u32[]{:S(2)}, u32[]{:S(2)}) collective-permute-start(bf16[4,160,128]{2,1,0:T(8,128)(2,1)S(1)} %slice.79), channel_id=1, source_target_pairs={{0,64},{8,72},{16,80},{24,88},{32,96},{40,104},{48,112},{56,120},{... | collective-permute-start | bytes 491528 | tf_op jit(solution)/shard_map/ppermute | solution.py:343
  158.5 10.4 %collective-permute-start.24 = (bf16[4,160,128]{2,1,0:T(8,128)(2,1)S(1)}, bf16[4,160,128]{2,1,0:T(8,128)(2,1)S(1)}, u32[]{:S(2)}, u32[]{:S(2)}) collective-permute-start(bf16[4,160,128]{2,1,0:T(8,128)(2,1)S(1)} %slice.78), channel_id=1, source_target_pairs={{0,192},{8,200},{16,208},{24,216},{32,224},{40,232},{48,240},{56,2... | collective-permute-start | bytes 491528 | tf_op jit(solution)/shard_map/ppermute | solution.py:343
  169.0 3.2 %collective-permute-start.27 = (bf16[8,640,128]{2,1,0:T(8,128)(2,1)S(1)}, bf16[8,640,128]{2,1,0:T(8,128)(2,1)S(1)}, u32[]{:S(2)}, u32[]{:S(2)}) collective-permute-start(bf16[8,640,128]{2,1,0:T(8,128)(2,1)S(1)} %shard_map.135.mine_ref), channel_id=1, source_target_pairs={{0,8},{8,0},{16,24},{24,16},{32,40},{40,32},{48,56},{56,48},{64,72... | collective-permute-start | bytes 3932168 | tf_op jit(solution)/shard_map/ppermute | solution.py:364

commit v2 on v1

--- a/solution.py
+++ b/solution.py
@@ -411,7 +411,7 @@
             pltpu.VMEM((D, D), BF),
             pltpu.SemaphoreType.DMA((3,)),
         ],
-        compiler_params=pltpu.CompilerParams(vmem_limit_bytes=MEMORY),
+        compiler_params=pltpu.CompilerParams(vmem_limit_bytes=60 * 1024 * 1024),
     )(events, out_grad, out_weight)
     sent, quotient_shard, remainder_shard = together(sent, quotient_shard, remainder_shard)
     received = lax.all_to_all(sent, "ctx", 0, 0, tiled=True)

time: 177 us -> 176 us (level)
  starting transfers between devices: 74 us -> 81 us
  waiting for transfers between devices: 45.6 us -> 42.1 us
  local copies, waits for them, and re-layouts: 13.1 us -> 10.1 us
    ppermute x3, starting transfers between devices: 3.5 us -> 6.84 us  [scatter_sum(): total = total + lax.ppermute(sent, 'dp', turned(stride, 4, k))]
    unnamed x52 -> x46, local copies, waits for them, and re-layouts: 9.54 us -> 6.56 us
    ppermute x3, starting transfers between devices: 5.95 us -> 8.41 us  [over_z(): return [lax.ppermute(x, 'dp', turned(2, 4, k)) for k in (1, 2, 3)]]
  transfers between devices with their start and end apart: 32 -> 32, of which waited for: 15 -> 14; matrix products, arithmetic and copies ran while one was open for 4% -> 4% of each run, Pallas kernels for 20% -> 19%
where the time goes in v2:
time: 176 us; the launch traced here: 175 us
  starting transfers between devices  81 us (46%)
  waiting for transfers between devices  42.1 us (24%)
  Pallas kernels  36.8 us (21%)
  local copies, waits for them, and re-layouts  10.1 us (6%)
  between operations  3.29 us (2%)
    all_to_all x1, starting transfers between devices, body(): arrived = lax.all_to_all(packed, ('dp', 'ctx'), 0, 0, tiled=True)  15 us
    ppermute x7, starting transfers between devices, to_source(): held.append(lax.ppermute(sent, 'dp', turned(stride, size, k)))  14.9 us
    pallas_call x1, Pallas kernels, body(): call(backward_kernel, (out((NB, 4 * HD + 16, TOK), BF), out((HD, LEN), BF...  11.5 us
    ppermute x4, waiting for transfers between devices, over_y(): return lax.ppermute(x, 'dp', [(i, i ^ 8 * k) for i in range(32)])  10.7 us
    ppermute x9, starting transfers between devices, over_ctx(): return lax.ppermute(x, 'ctx', [(i, i ^ k) for i in range(8)])  9.66 us
    pallas_call x1, Pallas kernels, body(): call(forward_kernel, (out((4 * HD, LEN), BF), out((4 * HD, LEN), F32), ou...  9.04 us
    ppermute x3, starting transfers between devices, over_z(): return [lax.ppermute(x, 'dp', turned(2, 4, k)) for k in (1, 2, 3)]  8.41 us
    ppermute x9, waiting for transfers between devices, over_ctx(): return lax.ppermute(x, 'ctx', [(i, i ^ k) for i in range(8)])  7.55 us
  transfers between devices with their start and end apart: 32, of which 14 were waited for; matrix products, arithmetic and copies ran while one was open for 4% of the time, Pallas kernels for 19%

profile of v2, /device:TPU:1, one launch (start us, length us, event | category | flops | bytes accessed | tf_op | source)
XLA Modules:
  0.0 174.9 jit_solution(14368968223524069577)
XLA Ops:
  0.6 2.6 %collective-permute-start = (bf16[256,512]{1,0:T(8,128)(2,1)}, bf16[256,512]{1,0:T(8,128)(2,1)S(1)}, u32[]{:S(2)}, u32[]{:S(2)}) collective-permute-start(bf16[256,512]{1,0:T(8,128)(2,1)} %og_ref.1), channel_id=1, source_target_pairs={{0,1},{1,0},{2,3},{3,2},{4,5},{5,4},{6,7},{7,6},{8,9},{9,8},{10,11... | collective-permute-start | bytes 786440 | tf_op jit(solution)/shard_map/ppermute | solution.py:347
  3.2 3.0 %shard_map.129 = bf16[8,288,512]{2,1,0:T(8,128)(2,1)} custom-call(bf16[256,512]{1,0:T(8,128)(2,1)} %ev_hbm.1, bf16[256,512]{1,0:T(8,128)(2,1)} %og_ref.1, bf16[512,512]{1,0:T(8,128)(2,1)} %wo_hbm.1), custom_call_target="tpu_custom_call" | custom-call | tf_op jit(solution)/shard_map/pallas_call | solution.py:403
  6.3 4.5 %all-to-all-start = ((bf16[8,288,512]{2,1,0:T(8,128)(2,1)}), bf16[8,288,512]{2,1,0:T(8,128)(2,1)}, u32[]{:S(2)}, u32[]{:S(2)}) async-start(bf16[8,288,512]{2,1,0:T(8,128)(2,1)} %shard_map.129), calls=%async_computation | async-start | bytes 4718592 | tf_op jit(solution)/shard_map/all_to_all | solution.py:417
  10.8 0.1 convert_reduce_fusion
  11.0 0.2 select_reduce_fusion
  11.2 0.1 sub.47
  11.4 0.1 select_reduce_fusion.1
  11.5 0.1 sub.45
  11.9 1.0 collective-permute-start.1
  13.3 2.5 %copy.64 = bf16[512,2048]{0,1:T(8,128)(2,1)} copy(bf16[512,2048]{1,0:T(8,128)(2,1)S(1)} %copy-done.6) | data formatting | bytes 4194304 | tf_op args[2]
  15.8 0.6 fusion.14
  18.3 0.7 select_select_fusion
  19.0 1.0 dynamic-slice_bitcast_fusion.1
  20.0 0.2 broadcast_select_fusion.lo_ref
  20.4 1.4 collective-permute-start.4
  21.8 2.6 %collective-permute-start.3 = (s32[2,4,32]{2,1,0:T(4,128)S(1)}, s32[2,4,32]{2,1,0:T(4,128)S(1)}, u32[]{:S(2)}, u32[]{:S(2)}) collective-permute-start(s32[2,4,32]{2,1,0:T(4,128)S(1)} %get-tuple-element.102), channel_id=1, source_target_pairs={{0,128},{8,136},{16,144},{24,152},{32,160},{40,168},{48,176},{56,1... | collective-permute-start | bytes 3080 | tf_op jit(solution)/shard_map/ppermute | solution.py:317
  24.4 1.1 collective-permute-start.2
  25.5 1.8 %collective-permute-done.2 = s32[2,4,32]{2,1,0:T(4,128)S(1)} collective-permute-done((s32[2,4,32]{2,1,0:T(4,128)S(1)}, s32[2,4,32]{2,1,0:T(4,128)S(1)}, u32[]{:S(2)}, u32[]{:S(2)}) %collective-permute-start.2) | collective-permute-done | bytes 1056 | tf_op jit(solution)/shard_map/ppermute | solution.py:317
  27.4 6.5 %collective-permute-start.6 = (s32[4,2,32]{2,1,0:T(2,128)S(1)}, s32[4,2,32]{2,1,0:T(2,128)S(1)}, u32[]{:S(2)}, u32[]{:S(2)}) collective-permute-start(s32[4,2,32]{2,1,0:T(2,128)S(1)} %bitcast.162), channel_id=1, source_target_pairs={{0,32},{8,40},{16,48},{24,56},{32,0},{40,8},{48,16},{56,24},{64,96... | collective-permute-start | bytes 3080 | tf_op jit(solution)/shard_map/ppermute | solution.py:317
  33.8 2.4 %collective-permute-start.5 = (s32[4,2,32]{2,1,0:T(2,128)S(1)}, s32[4,2,32]{2,1,0:T(2,128)S(1)}, u32[]{:S(2)}, u32[]{:S(2)}) collective-permute-start(s32[4,2,32]{2,1,0:T(2,128)S(1)} %bitcast.160), channel_id=1, source_target_pairs={{0,16},{8,24},{16,32},{24,40},{32,48},{40,56},{48,0},{56,8},{64,80... | collective-permute-start | bytes 3080 | tf_op jit(solution)/shard_map/ppermute | solution.py:317
  36.2 3.5 %all-to-all-done.r_ref = bf16[8,288,512]{2,1,0:T(8,128)(2,1)} async-done(((bf16[8,288,512]{2,1,0:T(8,128)(2,1)}), bf16[8,288,512]{2,1,0:T(8,128)(2,1)}, u32[]{:S(2)}, u32[]{:S(2)}) %all-to-all-start) | async-done | bytes 2359328 | tf_op jit(solution)/shard_map/all_to_all | solution.py:417
  39.7 1.3 collective-permute-start.9
  41.0 9.0 %shard_map.130 = (bf16[256,2048]{1,0:T(8,128)(2,1)S(1)}, f32[256,2048]{1,0:T(8,128)}, f32[64,2048]{1,0:T(8,128)S(1)}, f32[8,4,2048]{2,1,0:T(4,128)}) custom-call(s32[4]{0:T(128)S(1)} %bitcast.139, bf16[8,288,512]{2,1,0:T(8,128)(2,1)} %all-to-all-done.r_ref, bf16[256,512]{1,0:T(8,128)(2,1)S(1)} %bitcast.138, s32[16,1,2048]{2,1,0:T(1,128)S(1)} %broadcast_select_fusion.lo_ref), custom_call_target="tpu_custom_call" | custom-call | tf_op jit(solution)/shard_map/pallas_call | solution.py:444
  50.0 1.0 copy-done.1
  51.0 4.2 %all-to-all-start.1 = ((f32[8,4,2048]{2,1,0:T(4,128)}), f32[8,4,2048]{2,1,0:T(4,128)S(1)}, u32[]{:S(2)}, u32[]{:S(2)}) async-start(f32[8,4,2048]{2,1,0:T(4,128)} %get-tuple-element.52), calls=%async_computation.1 | async-start | bytes 524288 | tf_op jit(solution)/shard_map/all_to_all | solution.py:452
  55.4 0.3 copy.67
  55.7 5.6 %all-to-all-done.1.st_ref = f32[8,4,2048]{2,1,0:T(4,128)S(1)} async-done(((f32[8,4,2048]{2,1,0:T(4,128)}), f32[8,4,2048]{2,1,0:T(4,128)S(1)}, u32[]{:S(2)}, u32[]{:S(2)}) %all-to-all-start.1) | async-done | bytes 262176 | tf_op jit(solution)/shard_map/all_to_all | solution.py:452
  61.4 0.3 collective-permute-start.11
  61.7 1.1 collective-permute-start.10
  62.8 1.2 copy-done.2
  64.0 11.5 %shard_map.131 = (bf16[8,272,256]{2,1,0:T(8,128)(2,1)}, bf16[64,2048]{1,0:T(8,128)(2,1)S(1)}) custom-call(s32[4]{0:T(128)S(1)} %bitcast.140, f32[8,4,2048]{2,1,0:T(4,128)S(1)} %all-to-all-done.1.st_ref, bf16[8,288,512]{2,1,0:T(8,128)(2,1)} %all-to-all-done.r_ref, s32[16,1,2048]{2,1,0:T(1,128)S(1)} %broadcast_select_fusion.lo_ref, ...), custom_call_target="tpu_custom_call" | custom-call | tf_op jit(solution)/shard_map/pallas_call | solution.py:456
  75.5 0.7 copy-done.3
  76.2 3.7 %all-to-all-start.2 = ((bf16[8,272,256]{2,1,0:T(8,128)(2,1)}), bf16[8,272,256]{2,1,0:T(8,128)(2,1)S(1)}, u32[]{:S(2)}, u32[]{:S(2)}) async-start(bf16[8,272,256]{2,1,0:T(8,128)(2,1)} %get-tuple-element.65.gp_ref), calls=%async_computation.2 | async-start | bytes 2228224 | tf_op jit(solution)/shard_map/all_to_all | solution.py:471
  80.0 0.9 copy-done.4
  80.9 3.2 %shard_map.132 = f32[1280,128]{1,0:T(8,128)S(1)} custom-call(s32[1]{0:T(128)} %bitcast.45.place_ref, bf16[8,272,256]{2,1,0:T(8,128)(2,1)} %get-tuple-element.65.gp_ref, bf16[8,288,512]{2,1,0:T(8,128)(2,1)} %all-to-all-done.r_ref, bf16[64,2048]{1,0:T(8,128)(2,1)S(1)} %copy-done.4, bf16[2,256,512]{2,1,0:T(8,128)(2,1)S(1)} %pad_maximum_fusion.refs_0_, ...), custom_call_target="tpu_custom_call" | custom-call | tf_op jit(solution)/shard_map/pallas_call | solution.py:475
  84.2 7.3 %collective-permute-start.12 = (f32[640,128]{1,0:T(8,128)S(1)}, f32[640,128]{1,0:T(8,128)S(1)}, u32[]{:S(2)}, u32[]{:S(2)}) collective-permute-start(f32[640,128]{1,0:T(8,128)S(1)} %dynamic-slice_bitcast_fusion), channel_id=1, source_target_pairs={{0,8},{8,0},{16,24},{24,16},{32,40},{40,32},{48,56},{56,48},{64,72... | collective-permute-start | bytes 983048 | tf_op jit(solution)/shard_map/ppermute | solution.py:359
  91.5 1.3 collective-permute-done.12
  92.9 2.7 %collective-permute-start.15 = (f32[160,128]{1,0:T(8,128)S(1)}, f32[160,128]{1,0:T(8,128)S(1)}, u32[]{:S(2)}, u32[]{:S(2)}) collective-permute-start(f32[160,128]{1,0:T(8,128)S(1)} %get-tuple-element.91), channel_id=1, source_target_pairs={{0,192},{8,200},{16,208},{24,216},{32,224},{40,232},{48,240},{56,2... | collective-permute-start | bytes 245768 | tf_op jit(solution)/shard_map/ppermute | solution.py:304
  95.6 4.1 %collective-permute-start.14 = (f32[160,128]{1,0:T(8,128)S(1)}, f32[160,128]{1,0:T(8,128)S(1)}, u32[]{:S(2)}, u32[]{:S(2)}) collective-permute-start(f32[160,128]{1,0:T(8,128)S(1)} %get-tuple-element.92), channel_id=1, source_target_pairs={{0,128},{8,136},{16,144},{24,152},{32,160},{40,168},{48,176},{56,1... | collective-permute-start | bytes 245768 | tf_op jit(solution)/shard_map/ppermute | solution.py:304
  99.7 0.4 collective-permute-done.15
  100.1 2.1 %collective-permute-done.14 = f32[160,128]{1,0:T(8,128)S(1)} collective-permute-done((f32[160,128]{1,0:T(8,128)S(1)}, f32[160,128]{1,0:T(8,128)S(1)}, u32[]{:S(2)}, u32[]{:S(2)}) %collective-permute-start.14) | collective-permute-done | bytes 81952 | tf_op jit(solution)/shard_map/ppermute | solution.py:304
  102.2 5.8 %collective-permute-start.18 = (f32[160,128]{1,0:T(8,128)S(1)}, f32[160,128]{1,0:T(8,128)S(1)}, u32[]{:S(2)}, u32[]{:S(2)}) collective-permute-start(f32[160,128]{1,0:T(8,128)S(1)} %fusion.3), channel_id=1, source_target_pairs={{0,48},{8,56},{16,0},{24,8},{32,16},{40,24},{48,32},{56,40},{64,11... | collective-permute-start | bytes 245768 | tf_op jit(solution)/shard_map/ppermute | solution.py:309
  107.9 0.4 collective-permute-start.17
  108.3 2.3 %collective-permute-start.16 = (f32[160,128]{1,0:T(8,128)S(1)}, f32[160,128]{1,0:T(8,128)S(1)}, u32[]{:S(2)}, u32[]{:S(2)}) collective-permute-start(f32[160,128]{1,0:T(8,128)S(1)} %fusion.3), channel_id=1, source_target_pairs={{0,16},{8,24},{16,32},{24,40},{32,48},{40,56},{48,0},{56,8},{64,80... | collective-permute-start | bytes 245768 | tf_op jit(solution)/shard_map/ppermute | solution.py:309
  110.6 4.6 %shard_map.133 = bf16[256,16,128]{2,1,0:T(8,128)(2,1)} custom-call(bf16[8,272,256]{2,1,0:T(8,128)(2,1)S(1)} %all-to-all-done.2.back_ref, bf16[512,2048]{1,0:T(8,128)(2,1)} %w_ref.1, bf16[256,512]{1,0:T(8,128)(2,1)S(1)} %copy-done, s32[1,256]{1,0:T(1,128)S(1)} %bitcast.142, s32[1,256]{1,0:T(1,128)S(1)} %bitcast.141), custom_call_target="tpu_custom_call" | custom-call | tf_op jit(solution)/shard_map/pallas_call | solution.py:481
  115.1 0.9 collective-permute-done.17
  116.1 1.1 collective-permute-start.19
  117.2 1.8 %collective-permute-done.19 = bf16[160,128]{1,0:T(8,128)(2,1)S(1)} collective-permute-done((bf16[160,128]{1,0:T(8,128)(2,1)S(1)}, bf16[160,128]{1,0:T(8,128)(2,1)S(1)}, u32[]{:S(2)}, u32[]{:S(2)}) %collective-permute-start.19) | collective-permute-done | bytes 40992 | tf_op jit(solution)/shard_map/ppermute | solution.py:347
  119.0 15.0 %all-to-all-start.3 = ((bf16[256,16,128]{2,1,0:T(8,128)(2,1)}), bf16[256,16,128]{2,1,0:T(8,128)(2,1)S(1)}, u32[]{:S(2)}, u32[]{:S(2)}) async-start(bf16[256,16,128]{2,1,0:T(8,128)(2,1)} %shard_map.133), calls=%async_computation.3 | async-start | bytes 2097152 | tf_op jit(solution)/shard_map/all_to_all | solution.py:491
  134.0 2.7 %collective-permute-start.22 = (bf16[2,160,128]{2,1,0:T(8,128)(2,1)S(1)}, bf16[2,160,128]{2,1,0:T(8,128)(2,1)S(1)}, u32[]{:S(2)}, u32[]{:S(2)}) collective-permute-start(bf16[2,160,128]{2,1,0:T(8,128)(2,1)S(1)} %pad_maximum_fusion.2), channel_id=1, source_target_pairs={{0,6},{1,7},{2,4},{3,5},{4,2},{5,3},{6,0},{7,1},{8,14},{9,15},{10,... | collective-permute-start | bytes 245768 | tf_op jit(solution)/shard_map/ppermute | solution.py:347
  136.7 0.6 collective-permute-start.21
  137.4 5.4 %collective-permute-done.20 = bf16[2,160,128]{2,1,0:T(8,128)(2,1)S(1)} collective-permute-done((bf16[2,160,128]{2,1,0:T(8,128)(2,1)S(1)}, bf16[2,160,128]{2,1,0:T(8,128)(2,1)S(1)}, u32[]{:S(2)}, u32[]{:S(2)}) %collective-permute-start.20) | collective-permute-done | bytes 81952 | tf_op jit(solution)/shard_map/ppermute | solution.py:347
  142.8 0.3 collective-permute-done.21
  143.2 3.0 %collective-permute-start.25 = (bf16[8,160,128]{2,1,0:T(8,128)(2,1)S(1)}, bf16[8,160,128]{2,1,0:T(8,128)(2,1)S(1)}, u32[]{:S(2)}, u32[]{:S(2)}) collective-permute-start(bf16[8,160,128]{2,1,0:T(8,128)(2,1)S(1)} %constant_dynamic-update-slice_fusion.16.refs_0_), channel_id=1, source_target_pairs={{0,192},{8,200},{16,208},{24,216},{32,224},{40,232},{48,240},{56,2... | collective-permute-start | bytes 983048 | tf_op jit(solution)/shard_map/ppermute | solution.py:343
  146.4 10.6 %collective-permute-done.25.refs_4_ = bf16[8,160,128]{2,1,0:T(8,128)(2,1)S(1)} collective-permute-done((bf16[8,160,128]{2,1,0:T(8,128)(2,1)S(1)}, bf16[8,160,128]{2,1,0:T(8,128)(2,1)S(1)}, u32[]{:S(2)}, u32[]{:S(2)}) %collective-permute-start.25) | collective-permute-done | bytes 327712 | tf_op jit(solution)/shard_map/ppermute | solution.py:343
  157.1 1.0 collective-permute-start.26
  158.1 1.9 %collective-permute-start.24 = (bf16[4,160,128]{2,1,0:T(8,128)(2,1)S(1)}, bf16[4,160,128]{2,1,0:T(8,128)(2,1)S(1)}, u32[]{:S(2)}, u32[]{:S(2)}) collective-permute-start(bf16[4,160,128]{2,1,0:T(8,128)(2,1)S(1)} %slice.78), channel_id=1, source_target_pairs={{0,192},{8,200},{16,208},{24,216},{32,224},{40,232},{48,240},{56,2... | collective-permute-start | bytes 491528 | tf_op jit(solution)/shard_map/ppermute | solution.py:343
  160.0 0.1 copy.75
  160.3 0.1 copy.74
  160.5 5.7 %all-to-all-done.3.in_ref = bf16[256,16,128]{2,1,0:T(8,128)(2,1)S(1)} async-done(((bf16[256,16,128]{2,1,0:T(8,128)(2,1)}), bf16[256,16,128]{2,1,0:T(8,128)(2,1)S(1)}, u32[]{:S(2)}, u32[]{:S(2)}) %all-to-all-start.3) | async-done | bytes 1048608 | tf_op jit(solution)/shard_map/all_to_all | solution.py:491
  166.3 2.2 %shard_map.134 = (f32[512,512]{1,0:T(8,128)}, f32[512,512]{1,0:T(8,128)}) custom-call(bf16[256,16,128]{2,1,0:T(8,128)(2,1)S(1)} %all-to-all-done.3.in_ref, s32[512,1]{1,0:T(8,128)S(1)} %reshape_squeeze.8.qc_ref, s32[1,512]{1,0:T(1,128)S(1)} %bitcast.144, s32[512,1]{1,0:T(8,128)S(1)} %reshape_squeeze.9.rc_ref, s32[1,512]{1,0:T(1,128)S(1)} %bitcast.143), custom_call_target="tpu_custom_call" | custom-call | tf_op jit(solution)/shard_map/pallas_call | solution.py:497
  168.6 0.5 collective-permute-start.27
  169.1 2.7 %collective-permute-done.27.other_ref = bf16[8,640,128]{2,1,0:T(8,128)(2,1)S(1)} collective-permute-done((bf16[8,640,128]{2,1,0:T(8,128)(2,1)S(1)}, bf16[8,640,128]{2,1,0:T(8,128)(2,1)S(1)}, u32[]{:S(2)}, u32[]{:S(2)}) %collective-permute-start.27) | collective-permute-done | bytes 1310752 | tf_op jit(solution)/shard_map/ppermute | solution.py:364
  171.8 3.2 %shard_map.136 = (f32[512,2048]{1,0:T(8,128)}, f32[512,512]{1,0:T(8,128)}) custom-call(s32[1]{0:T(128)} %bitcast.64.core_ref, bf16[8,640,128]{2,1,0:T(8,128)(2,1)S(1)} %shard_map.135.mine_ref, bf16[8,640,128]{2,1,0:T(8,128)(2,1)S(1)} %collective-permute-done.27.other_ref), custom_call_target="tpu_custom_call" | custom-call | tf_op jit(solution)/shard_map/pallas_call | solution.py:366
  (111 shorter events, 2.2 us)
Async XLA Ops:
  0.6 35.6 %collective-permute-start = (bf16[256,512]{1,0:T(8,128)(2,1)}, bf16[256,512]{1,0:T(8,128)(2,1)S(1)}, u32[]{:S(2)}, u32[]{:S(2)}) collective-permute-start(bf16[256,512]{1,0:T(8,128)(2,1)} %og_ref.1), channel_id=1, source_target_pairs={{0,1},{1,0},{2,3},{3,2},{4,5},{5,4},{6,7},{7,6},{8,9},{9,8},{10,11... | collective-permute-start | bytes 786440 | tf_op jit(solution)/shard_map/ppermute | solution.py:347
  6.2 4.6 %copy-start.10 = (s32[256]{0:T(256)S(1)}, s32[256]{0:T(256)}, u32[]{:S(2)}) copy-start(s32[256]{0:T(256)} %param.19) | copy-start | bytes 3076
  6.2 4.6 %copy-start.7 = (s32[256]{0:T(256)S(1)}, s32[256]{0:T(256)}, u32[]{:S(2)}) copy-start(s32[256]{0:T(256)} %param.18) | copy-start | bytes 3076
  6.2 4.6 %copy-start.8 = (s32[256]{0:T(256)S(1)}, s32[256]{0:T(256)}, u32[]{:S(2)}) copy-start(s32[256]{0:T(256)} %param.16) | copy-start | bytes 3076
  6.2 4.9 %copy-start.11 = (s32[256]{0:T(256)S(1)}, s32[256]{0:T(256)}, u32[]{:S(2)}) copy-start(s32[256]{0:T(256)} %param.17) | copy-start | bytes 3076
  6.3 6.7 %copy-start.9 = (s32[16,16]{1,0:T(8,128)S(1)}, s32[16,16]{1,0:T(8,128)}, u32[]{:S(2)}) copy-start(s32[16,16]{1,0:T(8,128)} %param.15) | copy-start | bytes 3076
  6.3 7.0 %copy-start.6 = (bf16[512,2048]{1,0:T(8,128)(2,1)S(1)}, bf16[512,2048]{1,0:T(8,128)(2,1)}, u32[]{:S(2)}) copy-start(bf16[512,2048]{1,0:T(8,128)(2,1)} %w_ref.1) | copy-start | bytes 6291460
  6.3 33.4 %all-to-all-start = ((bf16[8,288,512]{2,1,0:T(8,128)(2,1)}), bf16[8,288,512]{2,1,0:T(8,128)(2,1)}, u32[]{:S(2)}, u32[]{:S(2)}) async-start(bf16[8,288,512]{2,1,0:T(8,128)(2,1)} %shard_map.129), calls=%async_computation | async-start | bytes 4718592 | tf_op jit(solution)/shard_map/all_to_all | solution.py:417
  11.9 8.4 %collective-permute-start.1 = (s32[4,4,32]{2,1,0:T(4,128)S(1)}, s32[4,4,32]{2,1,0:T(4,128)S(1)}, u32[]{:S(2)}, u32[]{:S(2)}) collective-permute-start(s32[4,4,32]{2,1,0:T(4,128)S(1)} %bitcast.158), channel_id=1, source_target_pairs={{0,8},{8,0},{16,24},{24,16},{32,40},{40,32},{48,56},{56,48},{64,72... | collective-permute-start | bytes 6152 | tf_op jit(solution)/shard_map/ppermute | solution.py:317
  13.2 2.5 %copy-start.5 = (s32[1,4]{1,0:T(1,128)S(1)}, s32[1,4]{1,0:T(1,128)}, u32[]{:S(2)}) copy-start(s32[1,4]{1,0:T(1,128)} %param.14) | copy-start | bytes 52
  15.8 23.9 %copy-start = (bf16[256,512]{1,0:T(8,128)(2,1)S(1)}, bf16[256,512]{1,0:T(8,128)(2,1)}, u32[]{:S(2)}) copy-start(bf16[256,512]{1,0:T(8,128)(2,1)} %og_ref.1) | copy-start | bytes 786436
  20.4 6.9 %collective-permute-start.4 = (s32[2,4,32]{2,1,0:T(4,128)S(1)}, s32[2,4,32]{2,1,0:T(4,128)S(1)}, u32[]{:S(2)}, u32[]{:S(2)}) collective-permute-start(s32[2,4,32]{2,1,0:T(4,128)S(1)} %get-tuple-element.101), channel_id=1, source_target_pairs={{0,64},{8,72},{16,80},{24,88},{32,96},{40,104},{48,112},{56,120},{... | collective-permute-start | bytes 3080 | tf_op jit(solution)/shard_map/ppermute | solution.py:317
  21.8 5.5 %collective-permute-start.3 = (s32[2,4,32]{2,1,0:T(4,128)S(1)}, s32[2,4,32]{2,1,0:T(4,128)S(1)}, u32[]{:S(2)}, u32[]{:S(2)}) collective-permute-start(s32[2,4,32]{2,1,0:T(4,128)S(1)} %get-tuple-element.102), channel_id=1, source_target_pairs={{0,128},{8,136},{16,144},{24,152},{32,160},{40,168},{48,176},{56,1... | collective-permute-start | bytes 3080 | tf_op jit(solution)/shard_map/ppermute | solution.py:317
  24.4 2.9 %collective-permute-start.2 = (s32[2,4,32]{2,1,0:T(4,128)S(1)}, s32[2,4,32]{2,1,0:T(4,128)S(1)}, u32[]{:S(2)}, u32[]{:S(2)}) collective-permute-start(s32[2,4,32]{2,1,0:T(4,128)S(1)} %get-tuple-element.103), channel_id=1, source_target_pairs={{0,192},{8,200},{16,208},{24,216},{32,224},{40,232},{48,240},{56,2... | collective-permute-start | bytes 3080 | tf_op jit(solution)/shard_map/ppermute | solution.py:317
  27.4 23.6 %collective-permute-start.6 = (s32[4,2,32]{2,1,0:T(2,128)S(1)}, s32[4,2,32]{2,1,0:T(2,128)S(1)}, u32[]{:S(2)}, u32[]{:S(2)}) collective-permute-start(s32[4,2,32]{2,1,0:T(2,128)S(1)} %bitcast.162), channel_id=1, source_target_pairs={{0,32},{8,40},{16,48},{24,56},{32,0},{40,8},{48,16},{56,24},{64,96... | collective-permute-start | bytes 3080 | tf_op jit(solution)/shard_map/ppermute | solution.py:317
  33.8 17.2 %collective-permute-start.7 = (s32[4,2,32]{2,1,0:T(2,128)S(1)}, s32[4,2,32]{2,1,0:T(2,128)S(1)}, u32[]{:S(2)}, u32[]{:S(2)}) collective-permute-start(s32[4,2,32]{2,1,0:T(2,128)S(1)} %bitcast.161), channel_id=1, source_target_pairs={{0,48},{8,56},{16,0},{24,8},{32,16},{40,24},{48,32},{56,40},{64,11... | collective-permute-start | bytes 3080 | tf_op jit(solution)/shard_map/ppermute | solution.py:317
  33.8 17.2 %collective-permute-start.5 = (s32[4,2,32]{2,1,0:T(2,128)S(1)}, s32[4,2,32]{2,1,0:T(2,128)S(1)}, u32[]{:S(2)}, u32[]{:S(2)}) collective-permute-start(s32[4,2,32]{2,1,0:T(2,128)S(1)} %bitcast.160), channel_id=1, source_target_pairs={{0,16},{8,24},{16,32},{24,40},{32,48},{40,56},{48,0},{56,8},{64,80... | collective-permute-start | bytes 3080 | tf_op jit(solution)/shard_map/ppermute | solution.py:317
  39.7 21.6 %collective-permute-start.9 = (bf16[2,256,512]{2,1,0:T(8,128)(2,1)S(1)}, bf16[2,256,512]{2,1,0:T(8,128)(2,1)S(1)}, u32[]{:S(2)}, u32[]{:S(2)}) collective-permute-start(bf16[2,256,512]{2,1,0:T(8,128)(2,1)S(1)} %pad_maximum_fusion.refs_0_), channel_id=1, source_target_pairs={{0,6},{1,7},{2,4},{3,5},{4,2},{5,3},{6,0},{7,1},{8,14},{9,15},{10,... | collective-permute-start | bytes 1572872 | tf_op jit(solution)/shard_map/ppermute | solution.py:347
  41.0 20.3 %collective-permute-start.8 = (bf16[2,256,512]{2,1,0:T(8,128)(2,1)S(1)}, bf16[2,256,512]{2,1,0:T(8,128)(2,1)S(1)}, u32[]{:S(2)}, u32[]{:S(2)}) collective-permute-start(bf16[2,256,512]{2,1,0:T(8,128)(2,1)S(1)} %pad_maximum_fusion.refs_0_), channel_id=1, source_target_pairs={{0,2},{1,3},{2,0},{3,1},{4,6},{5,7},{6,4},{7,5},{8,10},{9,11},{10,... | collective-permute-start | bytes 1572872 | tf_op jit(solution)/shard_map/ppermute | solution.py:347
  50.0 1.0 copy-start.1
  51.0 10.3 %all-to-all-start.1 = ((f32[8,4,2048]{2,1,0:T(4,128)}), f32[8,4,2048]{2,1,0:T(4,128)S(1)}, u32[]{:S(2)}, u32[]{:S(2)}) async-start(f32[8,4,2048]{2,1,0:T(4,128)} %get-tuple-element.52), calls=%async_computation.1 | async-start | bytes 524288 | tf_op jit(solution)/shard_map/all_to_all | solution.py:452
  61.4 14.9 %collective-permute-start.11 = (bf16[256,512]{1,0:T(8,128)(2,1)S(1)}, bf16[256,512]{1,0:T(8,128)(2,1)S(1)}, u32[]{:S(2)}, u32[]{:S(2)}) collective-permute-start(bf16[256,512]{1,0:T(8,128)(2,1)S(1)} %slice_bitcast_fusion), channel_id=1, source_target_pairs={{0,2},{1,3},{2,0},{3,1},{4,6},{5,7},{6,4},{7,5},{8,10},{9,11},{10,... | collective-permute-start | bytes 786440 | tf_op jit(solution)/shard_map/ppermute | solution.py:347
  61.7 14.6 %collective-permute-start.10 = (bf16[256,512]{1,0:T(8,128)(2,1)S(1)}, bf16[256,512]{1,0:T(8,128)(2,1)S(1)}, u32[]{:S(2)}, u32[]{:S(2)}) collective-permute-start(bf16[256,512]{1,0:T(8,128)(2,1)S(1)} %slice_bitcast_fusion.1), channel_id=1, source_target_pairs={{0,6},{1,7},{2,4},{3,5},{4,2},{5,3},{6,0},{7,1},{8,14},{9,15},{10,... | collective-permute-start | bytes 786440 | tf_op jit(solution)/shard_map/ppermute | solution.py:347
  62.8 1.2 copy-start.2
  75.5 0.7 copy-start.3
  76.2 25.9 %all-to-all-start.2 = ((bf16[8,272,256]{2,1,0:T(8,128)(2,1)}), bf16[8,272,256]{2,1,0:T(8,128)(2,1)S(1)}, u32[]{:S(2)}, u32[]{:S(2)}) async-start(bf16[8,272,256]{2,1,0:T(8,128)(2,1)} %get-tuple-element.65.gp_ref), calls=%async_computation.2 | async-start | bytes 2228224 | tf_op jit(solution)/shard_map/all_to_all | solution.py:471
  80.0 0.9 copy-start.4
  84.2 8.6 %collective-permute-start.12 = (f32[640,128]{1,0:T(8,128)S(1)}, f32[640,128]{1,0:T(8,128)S(1)}, u32[]{:S(2)}, u32[]{:S(2)}) collective-permute-start(f32[640,128]{1,0:T(8,128)S(1)} %dynamic-slice_bitcast_fusion), channel_id=1, source_target_pairs={{0,8},{8,0},{16,24},{24,16},{32,40},{40,32},{48,56},{56,48},{64,72... | collective-permute-start | bytes 983048 | tf_op jit(solution)/shard_map/ppermute | solution.py:359
  92.8 6.8 %collective-permute-start.13 = (f32[160,128]{1,0:T(8,128)S(1)}, f32[160,128]{1,0:T(8,128)S(1)}, u32[]{:S(2)}, u32[]{:S(2)}) collective-permute-start(f32[160,128]{1,0:T(8,128)S(1)} %get-tuple-element.90), channel_id=1, source_target_pairs={{0,64},{8,72},{16,80},{24,88},{32,96},{40,104},{48,112},{56,120},{... | collective-permute-start | bytes 245768 | tf_op jit(solution)/shard_map/ppermute | solution.py:304
  92.9 7.2 %collective-permute-start.15 = (f32[160,128]{1,0:T(8,128)S(1)}, f32[160,128]{1,0:T(8,128)S(1)}, u32[]{:S(2)}, u32[]{:S(2)}) collective-permute-start(f32[160,128]{1,0:T(8,128)S(1)} %get-tuple-element.91), channel_id=1, source_target_pairs={{0,192},{8,200},{16,208},{24,216},{32,224},{40,232},{48,240},{56,2... | collective-permute-start | bytes 245768 | tf_op jit(solution)/shard_map/ppermute | solution.py:304
  95.6 6.5 %collective-permute-start.14 = (f32[160,128]{1,0:T(8,128)S(1)}, f32[160,128]{1,0:T(8,128)S(1)}, u32[]{:S(2)}, u32[]{:S(2)}) collective-permute-start(f32[160,128]{1,0:T(8,128)S(1)} %get-tuple-element.92), channel_id=1, source_target_pairs={{0,128},{8,136},{16,144},{24,152},{32,160},{40,168},{48,176},{56,1... | collective-permute-start | bytes 245768 | tf_op jit(solution)/shard_map/ppermute | solution.py:304
  102.2 13.0 %collective-permute-start.18 = (f32[160,128]{1,0:T(8,128)S(1)}, f32[160,128]{1,0:T(8,128)S(1)}, u32[]{:S(2)}, u32[]{:S(2)}) collective-permute-start(f32[160,128]{1,0:T(8,128)S(1)} %fusion.3), channel_id=1, source_target_pairs={{0,48},{8,56},{16,0},{24,8},{32,16},{40,24},{48,32},{56,40},{64,11... | collective-permute-start | bytes 245768 | tf_op jit(solution)/shard_map/ppermute | solution.py:309
  107.9 8.1 %collective-permute-start.17 = (f32[160,128]{1,0:T(8,128)S(1)}, f32[160,128]{1,0:T(8,128)S(1)}, u32[]{:S(2)}, u32[]{:S(2)}) collective-permute-start(f32[160,128]{1,0:T(8,128)S(1)} %fusion.3), channel_id=1, source_target_pairs={{0,32},{8,40},{16,48},{24,56},{32,0},{40,8},{48,16},{56,24},{64,96... | collective-permute-start | bytes 245768 | tf_op jit(solution)/shard_map/ppermute | solution.py:309
  108.3 7.7 %collective-permute-start.16 = (f32[160,128]{1,0:T(8,128)S(1)}, f32[160,128]{1,0:T(8,128)S(1)}, u32[]{:S(2)}, u32[]{:S(2)}) collective-permute-start(f32[160,128]{1,0:T(8,128)S(1)} %fusion.3), channel_id=1, source_target_pairs={{0,16},{8,24},{16,32},{24,40},{32,48},{40,56},{48,0},{56,8},{64,80... | collective-permute-start | bytes 245768 | tf_op jit(solution)/shard_map/ppermute | solution.py:309
  116.1 2.9 %collective-permute-start.19 = (bf16[160,128]{1,0:T(8,128)(2,1)S(1)}, bf16[160,128]{1,0:T(8,128)(2,1)S(1)}, u32[]{:S(2)}, u32[]{:S(2)}) collective-permute-start(bf16[160,128]{1,0:T(8,128)(2,1)S(1)} %add_convert_fusion), channel_id=1, source_target_pairs={{0,1},{1,0},{2,3},{3,2},{4,5},{5,4},{6,7},{7,6},{8,9},{9,8},{10,11... | collective-permute-start | bytes 122888 | tf_op jit(solution)/shard_map/ppermute | solution.py:347
  119.0 47.3 %all-to-all-start.3 = ((bf16[256,16,128]{2,1,0:T(8,128)(2,1)}), bf16[256,16,128]{2,1,0:T(8,128)(2,1)S(1)}, u32[]{:S(2)}, u32[]{:S(2)}) async-start(bf16[256,16,128]{2,1,0:T(8,128)(2,1)} %shard_map.133), calls=%async_computation.3 | async-start | bytes 2097152 | tf_op jit(solution)/shard_map/all_to_all | solution.py:491
  134.0 9.1 %collective-permute-start.22 = (bf16[2,160,128]{2,1,0:T(8,128)(2,1)S(1)}, bf16[2,160,128]{2,1,0:T(8,128)(2,1)S(1)}, u32[]{:S(2)}, u32[]{:S(2)}) collective-permute-start(bf16[2,160,128]{2,1,0:T(8,128)(2,1)S(1)} %pad_maximum_fusion.2), channel_id=1, source_target_pairs={{0,6},{1,7},{2,4},{3,5},{4,2},{5,3},{6,0},{7,1},{8,14},{9,15},{10,... | collective-permute-start | bytes 245768 | tf_op jit(solution)/shard_map/ppermute | solution.py:347
  136.7 6.4 %collective-permute-start.21 = (bf16[2,160,128]{2,1,0:T(8,128)(2,1)S(1)}, bf16[2,160,128]{2,1,0:T(8,128)(2,1)S(1)}, u32[]{:S(2)}, u32[]{:S(2)}) collective-permute-start(bf16[2,160,128]{2,1,0:T(8,128)(2,1)S(1)} %pad_maximum_fusion.2), channel_id=1, source_target_pairs={{0,4},{1,5},{2,6},{3,7},{4,0},{5,1},{6,2},{7,3},{8,12},{9,13},{10,... | collective-permute-start | bytes 245768 | tf_op jit(solution)/shard_map/ppermute | solution.py:347
  137.3 5.5 %collective-permute-start.20 = (bf16[2,160,128]{2,1,0:T(8,128)(2,1)S(1)}, bf16[2,160,128]{2,1,0:T(8,128)(2,1)S(1)}, u32[]{:S(2)}, u32[]{:S(2)}) collective-permute-start(bf16[2,160,128]{2,1,0:T(8,128)(2,1)S(1)} %pad_maximum_fusion.2), channel_id=1, source_target_pairs={{0,2},{1,3},{2,0},{3,1},{4,6},{5,7},{6,4},{7,5},{8,10},{9,11},{10,... | collective-permute-start | bytes 245768 | tf_op jit(solution)/shard_map/ppermute | solution.py:347
  143.2 13.9 %collective-permute-start.25 = (bf16[8,160,128]{2,1,0:T(8,128)(2,1)S(1)}, bf16[8,160,128]{2,1,0:T(8,128)(2,1)S(1)}, u32[]{:S(2)}, u32[]{:S(2)}) collective-permute-start(bf16[8,160,128]{2,1,0:T(8,128)(2,1)S(1)} %constant_dynamic-update-slice_fusion.16.refs_0_), channel_id=1, source_target_pairs={{0,192},{8,200},{16,208},{24,216},{32,224},{40,232},{48,240},{56,2... | collective-permute-start | bytes 983048 | tf_op jit(solution)/shard_map/ppermute | solution.py:343
  146.2 11.9 %collective-permute-start.23 = (bf16[8,160,128]{2,1,0:T(8,128)(2,1)S(1)}, bf16[8,160,128]{2,1,0:T(8,128)(2,1)S(1)}, u32[]{:S(2)}, u32[]{:S(2)}) collective-permute-start(bf16[8,160,128]{2,1,0:T(8,128)(2,1)S(1)} %constant_dynamic-update-slice_fusion.16.refs_0_), channel_id=1, source_target_pairs={{0,64},{8,72},{16,80},{24,88},{32,96},{40,104},{48,112},{56,120},{... | collective-permute-start | bytes 983048 | tf_op jit(solution)/shard_map/ppermute | solution.py:343
  157.1 11.4 %collective-permute-start.26 = (bf16[4,160,128]{2,1,0:T(8,128)(2,1)S(1)}, bf16[4,160,128]{2,1,0:T(8,128)(2,1)S(1)}, u32[]{:S(2)}, u32[]{:S(2)}) collective-permute-start(bf16[4,160,128]{2,1,0:T(8,128)(2,1)S(1)} %slice.79), channel_id=1, source_target_pairs={{0,64},{8,72},{16,80},{24,88},{32,96},{40,104},{48,112},{56,120},{... | collective-permute-start | bytes 491528 | tf_op jit(solution)/shard_map/ppermute | solution.py:343
  158.1 10.4 %collective-permute-start.24 = (bf16[4,160,128]{2,1,0:T(8,128)(2,1)S(1)}, bf16[4,160,128]{2,1,0:T(8,128)(2,1)S(1)}, u32[]{:S(2)}, u32[]{:S(2)}) collective-permute-start(bf16[4,160,128]{2,1,0:T(8,128)(2,1)S(1)} %slice.78), channel_id=1, source_target_pairs={{0,192},{8,200},{16,208},{24,216},{32,224},{40,232},{48,240},{56,2... | collective-permute-start | bytes 491528 | tf_op jit(solution)/shard_map/ppermute | solution.py:343
  168.6 3.2 %collective-permute-start.27 = (bf16[8,640,128]{2,1,0:T(8,128)(2,1)S(1)}, bf16[8,640,128]{2,1,0:T(8,128)(2,1)S(1)}, u32[]{:S(2)}, u32[]{:S(2)}) collective-permute-start(bf16[8,640,128]{2,1,0:T(8,128)(2,1)S(1)} %shard_map.135.mine_ref), channel_id=1, source_target_pairs={{0,8},{8,0},{16,24},{24,16},{32,40},{40,32},{48,56},{56,48},{64,72... | collective-permute-start | bytes 3932168 | tf_op jit(solution)/shard_map/ppermute | solution.py:364
